TPU v7x, 128 devices: a whole 4x4x4 slice. The times are simulated.
128 devices in a mesh: ctx: 16 (over y, x), ch: 8 (over z, core).
Axes of the slice: x: 4, y: 4, z: 4, core: 2. Of those that a mesh axis runs over, the one named last changes fastest.
Arguments:
- query: bfloat16 [8192, 8192], P('ctx', 'ch'), may hold values from -6 to 6
- keys_in: bfloat16 [8192, 8192], P('ctx', 'ch'), may hold values from -6 to 6
- values_in: bfloat16 [8192, 8192], P('ctx', 'ch'), may hold values from -6 to 6
- short_taps: float32 [3, 3, 8192], P(None, None, 'ch'), may hold values from -3.5 to 3.5
- mode_rates: float32 [16, 8192], P(None, 'ch'), may hold values from 0.00012207031 to 0.05
- mode_residues: float32 [16, 8192], P(None, 'ch'), may hold values from -0.06629126 to 0.06629126
- out_weight: bfloat16 [8192, 8192], P('ctx', 'ch'), may hold values from -0.0625 to 0.0625
Outputs:
- mixed: bfloat16 [8192, 8192], P('ctx', 'ch')
All inputs are finite; a program needn't handle non-finite values.
Results may differ from a plain program's by a relative error of at most 0.018.
Values may be sent and summed in bfloat16 or wider, within the bound.
A program may use at most 128 MiB of HBM per device.

v0:
```python
import math

import jax
import jax.numpy as jnp
from jax import lax
from jax.sharding import PartitionSpec as P

TAPS = 3


HIGHEST = lax.Precision.HIGHEST


def passed_along(value, axis, steps):
    count = lax.axis_size(axis)
    first, last = (max(0, -steps), min(count, count - steps))
    return lax.ppermute(value, axis, [(source, source + steps) for source in range(first, last)])


def depthwise(padded, taps_block):
    channels = padded.shape[1]
    kernel = taps_block[::-1][:, None, :]
    result = lax.conv_general_dilated(
        padded[None],
        kernel,
        (1,),
        "VALID",
        dimension_numbers=("NWC", "WIO", "NWC"),
        feature_group_count=channels,
        precision=HIGHEST,
    )
    return result[0]


def block_setup(values, rates):
    length, channels = values.shape
    block = math.gcd(length, 256)
    block_count = length // block
    offsets = jnp.arange(block, dtype=jnp.float32)
    pieces = values.reshape(block_count, block, channels)
    tails = jnp.exp(-(block - offsets)[:, None, None] * rates[None])
    ends = jnp.einsum("jrc,bjc->brc", tails, pieces, precision=HIGHEST)
    return (block, block_count, offsets, pieces, ends)


def modal_conv(values, rates, residues, state_in):
    length, channels = values.shape
    block, block_count, offsets, pieces, ends = block_setup(values, rates)
    powers = jnp.exp(-offsets[:, None, None] * rates[None])
    lifted = jnp.exp(offsets[:, None, None] * rates[None])
    distance = jnp.arange(block)[:, None] - jnp.arange(block)[None, :]
    products = jnp.einsum("irc,jrc->cij", powers * residues[None], lifted, precision=HIGHEST)
    toeplitz = jnp.where(distance[None] >= 0, products, 0.0)
    inner = jnp.einsum("cij,bjc->bic", toeplitz, pieces, precision=HIGHEST)
    places = jnp.arange(block_count)
    spacing = places[:, None] - places[None, :] - 1
    spans = (block * jnp.maximum(spacing, 0)).astype(jnp.float32)
    carry_map = jnp.where(
        spacing[:, :, None, None] >= 0, jnp.exp(-spans[:, :, None, None] * rates[None, None]), 0.0
    )
    before = jnp.exp(-(block * places).astype(jnp.float32)[:, None, None] * rates[None])
    starts = (
        jnp.einsum("bkrc,krc->brc", carry_map, ends, precision=HIGHEST) + before * state_in[None]
    )
    outer = jnp.einsum("irc,brc->bic", powers, residues[None] * starts, precision=HIGHEST)
    return (inner + outer).reshape(length, channels)


def grouped(values, rates, residues, state_in):
    length, channels = values.shape
    group = math.gcd(channels, 64)
    if group == channels:
        return modal_conv(values, rates, residues, state_in)
    group_count = channels // group

    def split(array):
        return array.reshape(array.shape[0], group_count, group).transpose(1, 0, 2)

    outputs = lax.map(
        lambda parts: modal_conv(parts[0], parts[1], parts[2], parts[3]),
        (split(values), split(rates), split(residues), split(state_in)),
    )
    return outputs.transpose(1, 0, 2).reshape(length, channels)


def per_device(query, keys_in, values_in, short_taps, mode_rates, mode_residues, out_weight):
    rows_here, channels = query.shape
    keep = TAPS - 1
    rim_query, rim_keys, rim_values = passed_along(
        (query[rows_here - keep :], keys_in[rows_here - keep :], values_in[rows_here - keep :]),
        "ctx",
        1,
    )

    def featurize(rim, stream, index):
        padded = jnp.concatenate([rim, stream], 0).astype(jnp.float32)
        return depthwise(padded, short_taps[index]).astype(jnp.bfloat16)

    query_feat = featurize(rim_query, query, 0)
    keys_feat = featurize(rim_keys, keys_in, 1)
    values_feat = featurize(rim_values, values_in, 2)
    gated = (keys_feat.astype(jnp.float32) * values_feat.astype(jnp.float32)).astype(jnp.bfloat16)
    by_channel, query_channel = (
        lax.all_to_all(gated, "ctx", split_axis=1, concat_axis=0, tiled=True),
        lax.all_to_all(query_feat, "ctx", split_axis=1, concat_axis=0, tiled=True),
    )
    slot = by_channel.shape[1]
    offset = lax.axis_index("ctx") * slot
    rates_mine = lax.dynamic_slice_in_dim(mode_rates, offset, slot, 1)
    residues_mine = lax.dynamic_slice_in_dim(mode_residues, offset, slot, 1)
    state_zero = jnp.zeros(rates_mine.shape, jnp.float32)
    longconv = grouped(by_channel.astype(jnp.float32), rates_mine, residues_mine, state_zero)
    result_channel = (query_channel.astype(jnp.float32) * longconv).astype(jnp.bfloat16)
    result_tokens = lax.all_to_all(result_channel, "ctx", split_axis=0, concat_axis=1, tiled=True)
    full = lax.all_gather(result_tokens, "ch", axis=1, tiled=True)
    empty = jnp.zeros((rows_here, out_weight.shape[1]), jnp.float32)
    piece = lax.all_gather(out_weight, "ctx", axis=0, tiled=True)
    columns = lax.slice_in_dim(full, 0, piece.shape[0], axis=1)
    total = empty + jnp.dot(columns, piece, preferred_element_type=jnp.float32)
    return total.astype(jnp.bfloat16)


def solution(mesh):
    in_specs = (
        P("ctx", "ch"),
        P("ctx", "ch"),
        P("ctx", "ch"),
        P(None, None, "ch"),
        P(None, "ch"),
        P(None, "ch"),
        P("ctx", "ch"),
    )
    out_specs = P("ctx", "ch")
    return jax.shard_map(
        per_device, mesh=mesh, in_specs=in_specs, out_specs=out_specs, check_vma=False
    )
```

profile of v0, /device:TPU:1, one launch (start us, length us, event | category | flops | bytes accessed | tf_op | source)
XLA Modules:
  0.0 303.3 jit_solution(8339514230207380846)
XLA Ops:
  7.3 3.9 %collective-permute-start.2 = (bf16[2,1024]{1,0:T(2,128)(2,1)S(1)}, bf16[2,1024]{1,0:T(2,128)(2,1)S(1)}, u32[]{:S(2)}, u32[]{:S(2)}) collective-permute-start(bf16[2,1024]{1,0:T(2,128)(2,1)S(1)} %slice.22), channel_id=1, source_target_pairs={{0,8},{8,16},{16,24},{24,32},{32,40},{40,48},{48,56},{56,64},{64,7... | collective-permute-start | bytes 12296 | tf_op jit(solution)/shard_map/ppermute | solution.py:17
  11.9 3.1 %collective-permute-start.1 = (bf16[2,1024]{1,0:T(2,128)(2,1)S(1)}, bf16[2,1024]{1,0:T(2,128)(2,1)S(1)}, u32[]{:S(2)}, u32[]{:S(2)}) collective-permute-start(bf16[2,1024]{1,0:T(2,128)(2,1)S(1)} %slice.20), channel_id=1, source_target_pairs={{0,8},{8,16},{16,24},{24,32},{32,40},{40,48},{48,56},{56,64},{64,7... | collective-permute-start | bytes 12296 | tf_op jit(solution)/shard_map/ppermute | solution.py:17
  15.8 2.8 collective-permute-start
  19.5 0.8 constant_dynamic-slice_fusion
  21.5 1.5 maximum_bitcast_fusion.2
  24.1 1.0 copy-done
  27.0 1.5 select_convert_fusion
  28.4 1.7 multiply_convert_fusion
  31.2 1.3 copy.27
  32.5 6.5 %all-to-all-start.1 = ((bf16[512,16,64]{0,2,1:T(8,128)(2,1)}), bf16[512,16,64]{0,2,1:T(8,128)(2,1)S(1)}, u32[]{:S(2)}, u32[]{:S(2)}) async-start(bf16[512,16,64]{0,2,1:T(8,128)(2,1)} %bitcast.16), calls=%async_computation.1 | async-start | bytes 2097152 | tf_op jit(solution)/shard_map/all_to_all | solution.py:104
  39.0 16.8 %fusion.28 = f32[64,256,256]{2,1,0:T(8,128)} fusion(f32[16,64]{0,1:T(8,128)S(1)} %copy.30, f32[16,64]{0,1:T(8,128)S(1)} %copy.29, f32[256]{0:T(256)S(1)} %iota_negate_fusion), kind=kOutput, calls=%fused_computation.38 | convolution fusion | flops 806092800 | bytes 16786432 | tf_op jit(solution)/shard_map/irc,jrc->cij/dot_general | solution.py:52
  57.4 1.5 select_convert_fusion.2
  59.9 1.3 copy.19
  61.3 6.7 %all-to-all-start = ((bf16[512,16,64]{0,2,1:T(8,128)(2,1)}), bf16[512,16,64]{0,2,1:T(8,128)(2,1)}, u32[]{:S(2)}, u32[]{:S(2)}) async-start(bf16[512,16,64]{0,2,1:T(8,128)(2,1)} %bitcast.6), calls=%async_computation | async-start | bytes 2097152 | tf_op jit(solution)/shard_map/all_to_all | solution.py:105
  69.3 1.1 convolution_bitcast_fusion
  71.0 3.0 multiply_reduce_fusion
  74.3 12.5 %fusion = f32[64,32,256]{2,1,0:T(8,128)S(1)} fusion(bf16[32,256,64]{1,0,2:T(8,128)(2,1)S(1)} %reshape.91, f32[64,256,256]{2,1,0:T(8,128)} %fusion.28, pred[256,256]{1,0:T(8,128)(4,1)S(1)} %subtract_compare_fusion), kind=kOutput, calls=%fused_computation | convolution fusion | flops 1614807040 | bytes 19988480 | tf_op jit(solution)/shard_map/cij,bjc->bic/dot_general | solution.py:54
  86.8 3.9 %add_bitcast_fusion = f32[32,256,64]{1,0,2:T(8,128)} fusion(f32[64,32,256]{2,1,0:T(8,128)S(1)} %fusion, f32[16,64,32]{2,0,1:T(8,128)S(1)} %copy.41, f32[16,64]{0,1:T(8,128)S(1)} %copy.29, f32[256]{0:T(256)S(1)} %iota_negate_fusion, f32[32]{0:T(128)S(1)} %convert_negate_fusion.1, f32[16,64]{0,1:T(8,128)S(1)} %copy.30), kind=kOutput, calls=%fused_computation.15 | convolution fusion | flops 101580800 | bytes 4334720 | tf_op jit(solution)/shard_map/irc,brc->bic/dot_general | solution.py:65
  90.7 1.9 reshape.92
  92.6 2.4 fusion.7
  94.9 20.6 %all_to_all.39 = bf16[16,512,64]{1,2,0:T(8,128)(2,1)} all-to-all(bf16[16,512,64]{1,2,0:T(8,128)(2,1)S(1)} %fusion.7), channel_id=1, replica_groups=mesh['ctx'=16,'ch'=8] {'ctx'}, dimensions={0} | all-to-all | bytes 2097152 | tf_op jit(solution)/shard_map/all_to_all | solution.py:114
  116.3 51.6 %all-gather.3.cloned.1.call-done = bf16[512,8192]{0,1:T(8,128)(2,1)} async-done(((bf16[512,1024]{0,1:T(8,128)(2,1)}), bf16[512,8192]{0,1:T(8,128)(2,1)}) %all-gather.3.cloned.1.call-update) | async-done | bytes 8388624 | tf_op jit(solution)/shard_map/all_gather | solution.py:115
  167.9 112.9 %all-gather.5.cloned.1.call-done = bf16[8192,1024]{1,0:T(8,128)(2,1)} async-done(((bf16[512,1024]{1,0:T(8,128)(2,1)}), bf16[8192,1024]{1,0:T(8,128)(2,1)}) %all-gather.5.cloned.1.call-update) | async-done | bytes 16777232 | tf_op jit(solution)/shard_map/all_gather | solution.py:117
  280.8 15.6 %convolution_convert_fusion = bf16[512,1024]{1,0:T(8,128)(2,1)} fusion(bf16[512,8192]{0,1:T(8,128)(2,1)} %all-gather.3.cloned.1.call-done, bf16[8192,1024]{1,0:T(8,128)(2,1)} %all-gather.5.cloned.1.call-done), kind=kOutput, calls=%fused_computation.16 | convolution fusion | flops 8590458880 | bytes 26214400 | tf_op jit(solution)/shard_map/dot_general | solution.py:119
  (61 shorter events, 13.5 us)
Async XLA Ops:
  7.3 14.2 %collective-permute-start.2 = (bf16[2,1024]{1,0:T(2,128)(2,1)S(1)}, bf16[2,1024]{1,0:T(2,128)(2,1)S(1)}, u32[]{:S(2)}, u32[]{:S(2)}) collective-permute-start(bf16[2,1024]{1,0:T(2,128)(2,1)S(1)} %slice.22), channel_id=1, source_target_pairs={{0,8},{8,16},{16,24},{24,32},{32,40},{40,48},{48,56},{56,64},{64,7... | collective-permute-start | bytes 12296 | tf_op jit(solution)/shard_map/ppermute | solution.py:17
  11.9 12.1 %collective-permute-start.1 = (bf16[2,1024]{1,0:T(2,128)(2,1)S(1)}, bf16[2,1024]{1,0:T(2,128)(2,1)S(1)}, u32[]{:S(2)}, u32[]{:S(2)}) collective-permute-start(bf16[2,1024]{1,0:T(2,128)(2,1)S(1)} %slice.20), channel_id=1, source_target_pairs={{0,8},{8,16},{16,24},{24,32},{32,40},{40,48},{48,56},{56,64},{64,7... | collective-permute-start | bytes 12296 | tf_op jit(solution)/shard_map/ppermute | solution.py:17
  15.8 40.3 %collective-permute-start = (bf16[2,1024]{1,0:T(2,128)(2,1)S(1)}, bf16[2,1024]{1,0:T(2,128)(2,1)S(1)}, u32[]{:S(2)}, u32[]{:S(2)}) collective-permute-start(bf16[2,1024]{1,0:T(2,128)(2,1)S(1)} %slice.18), channel_id=1, source_target_pairs={{0,8},{8,16},{16,24},{24,32},{32,40},{40,48},{48,56},{56,64},{64,7... | collective-permute-start | bytes 12296 | tf_op jit(solution)/shard_map/ppermute | solution.py:17
  23.1 2.0 copy-start.2
  24.0 1.0 copy-start
  25.4 1.0 copy-start.5
  25.7 1.2 copy-start.1
  32.5 28.8 %all-to-all-start.1 = ((bf16[512,16,64]{0,2,1:T(8,128)(2,1)}), bf16[512,16,64]{0,2,1:T(8,128)(2,1)S(1)}, u32[]{:S(2)}, u32[]{:S(2)}) async-start(bf16[512,16,64]{0,2,1:T(8,128)(2,1)} %bitcast.16), calls=%async_computation.1 | async-start | bytes 2097152 | tf_op jit(solution)/shard_map/all_to_all | solution.py:104
  39.0 17.1 %copy-start.3 = (bf16[512,1024]{1,0:T(8,128)(2,1)S(1)}, bf16[512,1024]{1,0:T(8,128)(2,1)}, u32[]{:S(2)}) copy-start(bf16[512,1024]{1,0:T(8,128)(2,1)} %param.7) | copy-start | bytes 3145732
  56.4 1.0 copy-start.6
  61.3 31.3 %all-to-all-start = ((bf16[512,16,64]{0,2,1:T(8,128)(2,1)}), bf16[512,16,64]{0,2,1:T(8,128)(2,1)}, u32[]{:S(2)}, u32[]{:S(2)}) async-start(bf16[512,16,64]{0,2,1:T(8,128)(2,1)} %bitcast.6), calls=%async_computation | async-start | bytes 2097152 | tf_op jit(solution)/shard_map/all_to_all | solution.py:105
  68.0 99.9 %all-gather.3.cloned.1.call-start = ((), (), s32[]{:S(2)}) async-start(), calls=%async_computation.3 | async-start | bytes 9437184 | tf_op jit(solution)/shard_map/all_gather | solution.py:115
  68.3 1.0 copy-start.4
  115.6 165.3 %all-gather.5.cloned.1.call-start = ((), (), s32[]{:S(2)}) async-start(), calls=%async_computation.4 | async-start | bytes 17825792 | tf_op jit(solution)/shard_map/all_gather | solution.py:117
Sparse Core Ops, SparseCore 0:
  115.7 52.1 all-gather.2
  170.0 110.7 all-gather.4
where the time goes:
time: 304 us; the launch traced here: 303 us
  waiting for transfers between devices  165 us (54%)
  matrix products  54.5 us (18%)
  starting transfers between devices  23.6 us (8%)
  blocking collectives  20.6 us (7%)
  local copies, waits for them, and re-layouts  17.6 us (6%)
  between operations  13.9 us (5%)
  other arithmetic  8.07 us (3%)
    all_gather x1, waiting for transfers between devices, per_device(): piece = lax.all_gather(out_weight, 'ctx', axis=0, tiled=True)  113 us
    all_gather x1, waiting for transfers between devices, per_device(): full = lax.all_gather(result_tokens, 'ch', axis=1, tiled=True)  51.6 us
    all_to_all x1, blocking collectives, per_device(): lax.all_to_all(result_channel, 'ctx', split_axis=0, concat_axis=1, tiled=...  20.6 us
    dot_general x1, matrix products, modal_conv(): jnp.einsum('irc,jrc->cij', powers * residues[None], lifted, precision=HIG...  16.8 us
    dot_general x1, matrix products, per_device(): total = empty + jnp.dot(columns, piece, preferred_element_type=jnp.float32)  15.6 us
    dot_general x1, matrix products, modal_conv(): inner = jnp.einsum('cij,bjc->bic', toeplitz, pieces, precision=HIGHEST)  12.5 us
    ppermute x3, starting transfers between devices, passed_along(): lax.ppermute(value, axis, [(source, source + steps) for source in range(f...  9.85 us
    all_to_all x1, starting transfers between devices, per_device(): lax.all_to_all(query_feat, 'ctx', split_axis=1, concat_axis=0, tiled=True)  6.73 us
  transfers between devices with their start and end apart: 7, of which 2 were waited for; matrix products, arithmetic and copies ran while one was open for 20% of the time, Pallas kernels for 0%

commit v1 on v0

v1 whole, which is shorter than its diff:
```python
import functools

import jax
import jax.numpy as jnp
from jax import lax
from jax.experimental import pallas as pl
from jax.experimental.pallas import tpu as pltpu
from jax.sharding import PartitionSpec as P

MESH = pl.DeviceIdType.MESH
SIDE = 4
ORDER = 16
ROWS = 512
WIDTH = 1024
LANES = 128
TILES = WIDTH // LANES
SEGS = 8
STEPS = ROWS // SEGS
HALF = ROWS // 2
QUART = ROWS // 4
PAD = 8
HALO = 16
OFFS = (0, -1, 1, 2)
F32 = jnp.float32
BF16 = jnp.bfloat16


def rounded(value):
    return value.astype(BF16).astype(F32)


def kernel(
    q_ref, k_ref, v_ref, taps_ref, rates_ref, res_ref, w_ref, out_ref,
    wbuf, abuf, acc, streams, gbuf, ybuf, halo, dec, ends, inits, xstate, ystate,
    w_send, w_recv, a_send, a_recv, h_send, h_recv, s_send, s_recv, own_sem,
):
    ctx = lax.axis_index("ctx")
    ch = lax.axis_index("ch")
    cy, cx = ctx // SIDE, ctx % SIDE
    cz, core = ch // 2, ch % 2

    def mod(value):
        return lax.rem(value + 2 * SIDE, SIDE)

    def at_xy(y, x):
        return (mod(y) * SIDE + mod(x), ch)

    following = (lax.rem(ctx + 1, SIDE * SIDE), ch)
    previous = (lax.rem(ctx + SIDE * SIDE - 1, SIDE * SIDE), ch)
    sibling = (ctx, cz * 2 + 1 - core)

    def at_z(z):
        return (ctx, mod(z) * 2 + core)

    barrier = pltpu.get_barrier_semaphore()
    partners = [at_xy(cy, cx + d) for d in (1, 2, 3)] + [at_xy(cy + d, cx) for d in (1, 2, 3)]
    partners += [at_z(cz + 1), at_z(cz - 1), sibling, following, previous]
    for partner in partners:
        pl.semaphore_signal(barrier, inc=1, device_id=partner, device_id_type=MESH)

    own_copy = pltpu.make_async_copy(w_ref, wbuf.at[ctx], own_sem)
    own_copy.start()
    own_copy.wait()
    pl.semaphore_wait(barrier, len(partners))

    def halo_copy(index):
        source = (q_ref, k_ref, v_ref)[index]
        return pltpu.make_async_remote_copy(
            src_ref=source.at[pl.ds(ROWS - HALO, HALO)], dst_ref=halo.at[index],
            send_sem=h_send.at[index], recv_sem=h_recv.at[index],
            device_id=following, device_id_type=MESH)

    for index in (1, 2, 0):
        halo_copy(index).start()

    def slot(half, first, second):
        first, second = mod(first), mod(second)
        return second * SIDE + first if half == 0 else first * SIDE + second

    mine = ((cx, cy), (cy, cx))

    def device_of(half, first, second):
        return at_xy(second, first) if half == 0 else at_xy(first, second)

    def w_copy(half, stage, piece, kind, receiving):
        f0, s0 = mine[half]
        f, s = f0, s0
        if stage == 1:
            f = f0 + OFFS[piece]
        step = 1 if kind % 2 == 0 else -1
        if receiving:
            back = -step if kind < 2 else -2 * step
        else:
            back = 0 if kind < 2 else -step
        if stage == 0:
            f = f + back
            target = device_of(half, f0 + step, s0)
        else:
            s = s + back
            target = device_of(half, f0, s0 + step)
        start = half * HALF + (QUART if kind == 3 else 0)
        size = HALF if kind < 2 else QUART
        where = wbuf.at[slot(half, f, s), pl.ds(start, size)]
        index = half * 20 + (kind if stage == 0 else 4 + 4 * piece + kind)
        return pltpu.make_async_remote_copy(
            src_ref=where, dst_ref=where, send_sem=w_send.at[index], recv_sem=w_recv.at[index],
            device_id=target, device_id_type=MESH)

    def w_start(half, stage, piece, kind):
        w_copy(half, stage, piece, kind, False).start()

    def w_wait(half, stage, piece, kind):
        w_copy(half, stage, piece, kind, True).wait_recv()

    def w_own(stage):
        for half in (0, 1):
            for kind in (0, 1):
                w_start(half, stage, 0, kind)

    def w_first():
        for half in (0, 1):
            for kind in (0, 1):
                w_wait(half, 0, 0, kind)
                w_start(half, 0, 0, kind + 2)
                w_start(half, 1, kind + 1, 0)
                w_start(half, 1, kind + 1, 1)

    def w_second(piece):
        for half in (0, 1):
            for kind in (0, 1):
                w_wait(half, 1, piece, kind)
                w_start(half, 1, piece, kind + 2)

    def w_opposite():
        for half in (0, 1):
            for kind in (2, 3):
                w_wait(half, 0, 0, kind)
            w_start(half, 1, 3, 0)
            w_start(half, 1, 3, 1)

    def w_last(piece):
        for half in (0, 1):
            for kind in (2, 3):
                w_wait(half, 1, piece, kind)

    def a_copy(kind, receiving):
        start, size = 0, ROWS
        if kind < 4:
            step = 1 if kind % 2 == 0 else -1
            if receiving:
                back = -step if kind < 2 else -2 * step
            else:
                back = 0 if kind < 2 else -step
            if kind >= 2:
                start, size = (HALF if kind == 3 else 0), HALF
            block = mod(cz + back) * 2 + core
            target = at_z(cz + step)
        else:
            side = 1 - core if receiving else core
            block = mod(cz + OFFS[kind - 4]) * 2 + side
            target = sibling
        where = abuf.at[block, pl.ds(start, size)]
        return pltpu.make_async_remote_copy(
            src_ref=where, dst_ref=where, send_sem=a_send.at[kind], recv_sem=a_recv.at[kind],
            device_id=target, device_id_type=MESH)

    def state_copy(stage, distance, receiving):
        held = (xstate, ystate)[stage]
        position = (cx, cy)[stage]
        index = mod(position - distance) if receiving else position
        target = at_xy(cy, cx + distance) if stage == 0 else at_xy(cy + distance, cx)
        number = stage * 3 + distance - 1
        return pltpu.make_async_remote_copy(
            src_ref=held.at[index], dst_ref=held.at[index],
            send_sem=s_send.at[number], recv_sem=s_recv.at[number],
            device_id=target, device_id_type=MESH)

    w_own(0)
    w_own(1)

    dec[...] = jnp.exp(-rates_ref[...])

    def widen(index):
        source = (q_ref, k_ref, v_ref)[index]

        def body(tile, carry):
            lanes = pl.ds(pl.multiple_of(tile * LANES, LANES), LANES)
            streams[index, tile, pl.ds(PAD, ROWS), :] = source[:, lanes].astype(F32)
            return carry

        lax.fori_loop(0, TILES, body, 0)

    def widen_halo(index):
        halo_copy(index).wait_recv()
        keep = jnp.where(ctx > 0, 1.0, 0.0).astype(F32)

        def body(tile, carry):
            lanes = pl.ds(pl.multiple_of(tile * LANES, LANES), LANES)
            rim = halo[index, :, lanes].astype(F32)
            streams[index, tile, pl.ds(0, PAD), :] = rim[HALO - PAD:] * keep
            return carry

        lax.fori_loop(0, TILES, body, 0)

    widen(1)
    widen(2)
    widen(0)
    widen_halo(1)
    widen_halo(2)
    widen_halo(0)

    def spread(row):
        return jnp.broadcast_to(row, (SEGS, LANES))

    def strided(index, tile, start):
        return streams[index, tile, pl.ds(start, SEGS, stride=STEPS), :]

    def tap_rows(index, lanes):
        return [spread(taps_ref[pl.ds(index * 3 + j, 1), lanes]) for j in range(3)]

    def first_tile(tile, carry):
        lanes = pl.ds(pl.multiple_of(tile * LANES, LANES), LANES)
        decay = [spread(dec[pl.ds(r, 1), lanes]) for r in range(ORDER)]
        k_taps, v_taps = tap_rows(1, lanes), tap_rows(2, lanes)

        def step(i, held):
            k1, k2, v1, v2, states = held
            k0, v0 = strided(1, tile, PAD + i), strided(2, tile, PAD + i)
            kf = rounded(k_taps[0] * k0 + k_taps[1] * k1 + k_taps[2] * k2)
            vf = rounded(v_taps[0] * v0 + v_taps[1] * v1 + v_taps[2] * v2)
            gated = rounded(kf * vf)
            gbuf[tile, i] = gated
            states = tuple(decay[r] * states[r] + gated for r in range(ORDER))
            return k0, k1, v0, v1, states

        zero = jnp.zeros((SEGS, LANES), F32)
        start = (strided(1, tile, PAD - 1), strided(1, tile, PAD - 2),
                 strided(2, tile, PAD - 1), strided(2, tile, PAD - 2), (zero,) * ORDER)
        states = lax.fori_loop(0, STEPS, step, start, unroll=2)[4]
        for r in range(ORDER):
            ends[tile, pl.ds(r, SEGS, stride=ORDER), :] = states[r]
        return carry

    lax.fori_loop(0, TILES, first_tile, 0)

    def combine_tile(tile, carry):
        lanes = pl.ds(pl.multiple_of(tile * LANES, LANES), LANES)
        jump = jnp.exp(-float(STEPS) * rates_ref[:, lanes])
        state = jnp.zeros((ORDER, LANES), F32)
        for seg in range(SEGS):
            inits[tile, pl.ds(seg * ORDER, ORDER), :] = state
            state = jump * state + ends[tile, pl.ds(seg * ORDER, ORDER), :]
        xstate[cx, :, lanes] = state
        return carry

    lax.fori_loop(0, TILES, combine_tile, 0)
    for distance in (1, 3, 2):
        state_copy(0, distance, False).start()

    w_first()

    for distance in (1, 3, 2):
        state_copy(0, distance, True).wait_recv()

    def row_tile(tile, carry):
        lanes = pl.ds(pl.multiple_of(tile * LANES, LANES), LANES)
        jump = jnp.exp(-float(ROWS) * rates_ref[:, lanes])
        state = jnp.zeros((ORDER, LANES), F32)
        for position in range(SIDE):
            state = jump * state + xstate[position, :, lanes]
        ystate[cy, :, lanes] = state
        return carry

    lax.fori_loop(0, TILES, row_tile, 0)
    for distance in (1, 3, 2):
        state_copy(1, distance, False).start()

    w_second(0)

    for distance in (1, 3, 2):
        state_copy(1, distance, True).wait_recv()

    def seed_tile(tile, carry):
        lanes = pl.ds(pl.multiple_of(tile * LANES, LANES), LANES)
        rate = rates_ref[:, lanes]
        jump_x = jnp.exp(-float(ROWS) * rate)
        jump_y = jnp.exp(-float(ROWS * SIDE) * rate)
        before_x = jnp.zeros((ORDER, LANES), F32)
        before_y = jnp.zeros((ORDER, LANES), F32)
        for position in range(SIDE - 1):
            before_x = jnp.where(position < cx, jump_x * before_x + xstate[position, :, lanes], before_x)
            before_y = jnp.where(position < cy, jump_y * before_y + ystate[position, :, lanes], before_y)
        shift = (cx * ROWS).astype(F32)
        state = before_x + jnp.exp(-shift * rate) * before_y
        jump = jnp.exp(-float(STEPS) * rate)
        for seg in range(SEGS):
            rows = pl.ds(seg * ORDER, ORDER)
            inits[tile, rows, :] = inits[tile, rows, :] + state
            state = jump * state
        return carry

    lax.fori_loop(0, TILES, seed_tile, 0)

    def second_tile(tile, carry):
        lanes = pl.ds(pl.multiple_of(tile * LANES, LANES), LANES)
        decay = [spread(dec[pl.ds(r, 1), lanes]) for r in range(ORDER)]
        weight = [spread(res_ref[pl.ds(r, 1), lanes]) for r in range(ORDER)]
        q_taps = tap_rows(0, lanes)

        def step(i, held):
            q1, q2, states = held
            q0 = strided(0, tile, PAD + i)
            qf = rounded(q_taps[0] * q0 + q_taps[1] * q1 + q_taps[2] * q2)
            gated = gbuf[tile, i]
            states = tuple(decay[r] * states[r] + gated for r in range(ORDER))
            terms = [weight[r] * states[r] for r in range(ORDER)]
            while len(terms) > 1:
                terms = [terms[j] + terms[j + 1] for j in range(0, len(terms), 2)]
            ybuf[pl.ds(i, SEGS, stride=STEPS), :] = qf * terms[0]
            return q0, q1, states

        start = (strided(0, tile, PAD - 1), strided(0, tile, PAD - 2),
                 tuple(inits[tile, pl.ds(r, SEGS, stride=ORDER), :] for r in range(ORDER)))
        lax.fori_loop(0, STEPS, step, start, unroll=2)
        abuf[ch, :, lanes] = ybuf[...].astype(BF16)
        return carry

    lax.fori_loop(0, TILES, second_tile, 0)

    for kind in (0, 1, 4):
        a_copy(kind, False).start()

    w_opposite()
    w_last(0)

    for kind in (0, 1):
        a_copy(kind, True).wait_recv()
        a_copy(kind + 2, False).start()
        a_copy(kind + 5, False).start()

    w_second(1)
    w_second(2)

    for kind in (2, 3):
        a_copy(kind, True).wait_recv()
    a_copy(7, False).start()
    acc[...] = jnp.zeros_like(acc)
    for kind in (4, 5, 6, 7):
        a_copy(kind, True).wait_recv()

    def multiply(dy, dx):
        y, x = mod(cy + dy), mod(cx + dx)
        shard = y * SIDE + x
        block = shard // 2
        columns = pl.ds(pl.multiple_of((shard % 2) * ROWS, ROWS), ROWS)

        def body(chunk, carry):
            lanes = pl.ds(pl.multiple_of(chunk * HALF, HALF), HALF)
            acc[:, lanes] += jnp.dot(
                abuf[block, :, columns], wbuf[shard, :, lanes], preferred_element_type=F32)
            return carry

        lax.fori_loop(0, WIDTH // HALF, body, 0)

    def near(t, carry):
        multiply(t // 3 - 1, t % 3 - 1)
        return carry

    lax.fori_loop(0, 9, near, 0)

    w_second(3)

    def straight(t, carry):
        multiply(2 * t, 2 - 2 * t)
        return carry

    lax.fori_loop(0, 2, straight, 0)

    w_last(1)
    w_last(2)

    def slanted(t, carry):
        across = t // 2
        sign = 2 * (t % 2) - 1
        multiply(2 * across + sign * (1 - across), 2 * (1 - across) + sign * across)
        return carry

    lax.fori_loop(0, 4, slanted, 0)

    w_last(3)

    def final(t, carry):
        multiply(2 + t, 2)
        return carry

    lax.fori_loop(0, 1, final, 0)
    out_ref[...] = acc[...].astype(BF16)

    for half in (0, 1):
        for kind in range(4):
            w_copy(half, 0, 0, kind, False).wait_send()
            for piece in range(4):
                w_copy(half, 1, piece, kind, False).wait_send()
    for kind in range(8):
        a_copy(kind, False).wait_send()
    for index in range(3):
        halo_copy(index).wait_send()
    for stage in range(2):
        for distance in (1, 2, 3):
            state_copy(stage, distance, False).wait_send()


def per_device(query, keys_in, values_in, short_taps, mode_rates, mode_residues, out_weight):
    vmem = pl.BlockSpec(memory_space=pltpu.VMEM)
    dma = pltpu.SemaphoreType.DMA
    return pl.pallas_call(
        kernel,
        out_shape=jax.ShapeDtypeStruct((ROWS, WIDTH), BF16),
        in_specs=[vmem] * 6 + [pl.BlockSpec(memory_space=pl.ANY)],
        out_specs=vmem,
        scratch_shapes=[
            pltpu.VMEM((SIDE * SIDE, ROWS, WIDTH), BF16),
            pltpu.VMEM((8, ROWS, WIDTH), BF16),
            pltpu.VMEM((ROWS, WIDTH), F32),
            pltpu.VMEM((3, TILES, PAD + ROWS, LANES), F32),
            pltpu.VMEM((TILES, STEPS, SEGS, LANES), F32),
            pltpu.VMEM((ROWS, LANES), F32),
            pltpu.VMEM((3, HALO, WIDTH), BF16),
            pltpu.VMEM((ORDER, WIDTH), F32),
            pltpu.VMEM((TILES, SEGS * ORDER, LANES), F32),
            pltpu.VMEM((TILES, SEGS * ORDER, LANES), F32),
            pltpu.VMEM((SIDE, ORDER, WIDTH), F32),
            pltpu.VMEM((SIDE, ORDER, WIDTH), F32),
            dma((40,)), dma((40,)), dma((8,)), dma((8,)), dma((3,)), dma((3,)), dma((6,)), dma((6,)),
            dma,
        ],
        compiler_params=pltpu.CompilerParams(
            collective_id=0, has_side_effects=True, vmem_limit_bytes=56 * 1024 * 1024),
        cost_estimate=pl.CostEstimate(
            flops=2 * ROWS * 8192 * WIDTH, bytes_accessed=6 * 1024 * 1024, transcendentals=0),
    )(query, keys_in, values_in, short_taps.reshape(9, WIDTH), mode_rates, mode_residues, out_weight)


def solution(mesh):
    in_specs = (
        P("ctx", "ch"),
        P("ctx", "ch"),
        P("ctx", "ch"),
        P(None, None, "ch"),
        P(None, "ch"),
        P(None, "ch"),
        P("ctx", "ch"),
    )
    return jax.shard_map(
        per_device, mesh=mesh, in_specs=in_specs, out_specs=P("ctx", "ch"), check_vma=False
    )
```

time: 304 us -> 140 us (0.46)
  waiting for transfers between devices: 165 us -> 0 us
  Pallas kernels: 0 us -> 136 us
  matrix products: 54.5 us -> 0 us
  starting transfers between devices: 23.6 us -> 0 us
  blocking collectives: 20.6 us -> 0 us
  local copies, waits for them, and re-layouts: 17.6 us -> 3.71 us
  between operations: 13.9 us -> 0.01 us
  other arithmetic: 8.07 us -> 0 us
    all_gather x2 -> x0, waiting for transfers between devices: 165 us -> none  [the longest x1 113 us: per_device(): piece = lax.all_gather(out_weight, 'ctx', axis=0, tiled=True)]
    pallas_call x0 -> x1, Pallas kernels: none -> 136 us  [per_device(): pl.pallas_call(kernel, out_shape=jax.ShapeDtypeStruct((ROWS, WIDTH), BF16...]
    dot_general x5 -> x0, matrix products: 49.9 us -> none  [the longest x1 16.8 us: modal_conv(): jnp.einsum('irc,jrc->cij', powers * residues[None], lifted, precision=HIG...]
    all_to_all x1 -> x0, blocking collectives: 20.6 us -> none  [per_device(): lax.all_to_all(result_channel, 'ctx', split_axis=0, concat_axis=1, tiled=...]
    all_to_all x2 -> x0, starting transfers between devices: 13.2 us -> none  [the longest x1 6.73 us: per_device(): lax.all_to_all(query_feat, 'ctx', split_axis=1, concat_axis=0, tiled=True)]
    ppermute x3 -> x0, starting transfers between devices: 9.85 us -> none  [passed_along(): lax.ppermute(value, axis, [(source, source + steps) for source in range(f...]
    convert_element_type x8 -> x0, local copies, waits for them, and re-layouts: 4.67 us -> none  [the longest x4 2.34 us: featurize(): return depthwise(padded, short_taps[index]).astype(jnp.bfloat16)]
    conv_general_dilated x3 -> x0, matrix products: 4.66 us -> none  [depthwise(): lax.conv_general_dilated(padded[None], kernel, (1,), 'VALID', dimension_n...]
  transfers between devices with their start and end apart: 7 -> 0, of which waited for: 2 -> 0; matrix products, arithmetic and copies ran while one was open for 20% -> 0% of each run, Pallas kernels for 0% -> 0%
where the time goes in v1:
time: 140 us
  Pallas kernels  136 us (97%)
  local copies, waits for them, and re-layouts  3.71 us (3%)
    pallas_call x1, Pallas kernels, per_device(): pl.pallas_call(kernel, out_shape=jax.ShapeDtypeStruct((ROWS, WIDTH), BF16...  136 us

profile of v1, /device:TPU:1, one launch (start us, length us, event | category | flops | bytes accessed | tf_op | source)
XLA Modules:
  0.0 139.7 jit_solution(2115980303003476313)
XLA Ops:
  0.0 1.4 %reshape.3.taps_ref = f32[9,1024]{1,0:T(8,128)} reshape(f32[3,3,1024]{2,1,0:T(4,128)} %param.10) | data formatting | bytes 73728 | tf_op jit(solution)/shard_map/reshape | solution.py:441
  1.4 136.0 %shard_map.73 = bf16[512,1024]{1,0:T(8,128)(2,1)} custom-call(bf16[512,1024]{1,0:T(8,128)(2,1)} %q_ref.1, bf16[512,1024]{1,0:T(8,128)(2,1)} %k_ref.1, bf16[512,1024]{1,0:T(8,128)(2,1)} %v_ref.1, f32[9,1024]{1,0:T(8,128)} %reshape.3.taps_ref, f32[16,1024]{1,0:T(8,128)} %rates_ref.1, f32[16,1024]{1,0:T(8,128)} %res_ref.1, bf16[512,1024]{1,0:T(8,128)(2,1)} %w_ref.1), custom_call_target="tpu_custom_call" | custom-call | flops 8589934592 | bytes 6291456 | tf_op jit(solution)/shard_map/pallas_call | solution.py:416
  137.4 2.3 %copy.9 = bf16[512,1024]{1,0:T(8,128)(2,1)} copy(bf16[512,1024]{1,0:T(8,128)(2,1)} %shard_map.73) | data formatting | bytes 2097152

commit v2 on v0

v2 whole, which is shorter than its diff:
```python
import jax
import jax.numpy as jnp
from jax import lax
from jax.experimental import pallas as pl
from jax.experimental.pallas import tpu as pltpu
from jax.sharding import PartitionSpec as P

MESH = pl.DeviceIdType.MESH
SIDE = 4
ORDER = 16
ROWS = 512
WIDTH = 1024
LANES = 128
TILES = WIDTH // LANES
SEGS = 8
STEPS = ROWS // SEGS
PAD = 8
HALO = 16
PARTS = 2
PART = WIDTH // PARTS
CHUNKS = 4
CHUNK = WIDTH // CHUNKS
CUT = 224
OFFS = (0, -1, 1, 2)
PER_CHUNK = 17
F32 = jnp.float32
BF16 = jnp.bfloat16


def rounded(value):
    return value.astype(BF16).astype(F32)


def kernel(
    q_hbm, k_hbm, v_hbm, taps_ref, rates_ref, res_ref, w_ref, out_ref,
    wbuf, abuf, acc, cout, cin, inputs, streams, gbuf, ybuf, halo, dec, ends, inits, xstate, ystate,
    w_send, w_recv, a_send, a_recv, p_send, p_recv, c_send, c_recv, h_send, h_recv, s_send, s_recv,
    own_sem, in_sem,
):
    ctx = lax.axis_index("ctx")
    ch = lax.axis_index("ch")
    cy, cx = ctx // SIDE, ctx % SIDE
    cz, core = ch // 2, ch % 2
    column, side = cx % 2, cx // 2
    role = jnp.where(core == side, 0, 1)

    def mod(value):
        return lax.rem(value + 2 * SIDE, SIDE)

    def at_xy(y, x):
        return (mod(y) * SIDE + mod(x), ch)

    following = (lax.rem(ctx + 1, SIDE * SIDE), ch)
    previous = (lax.rem(ctx + SIDE * SIDE - 1, SIDE * SIDE), ch)
    sibling = (ctx, cz * 2 + 1 - core)
    beside = at_xy(cy, cx + 1 - 2 * column)
    partner = at_xy(cy, 3 - cx)
    crossed = (cy * SIDE + 3 - cx, cz * 2 + 1 - core)

    def at_z(z):
        return (ctx, mod(z) * 2 + core)

    barrier = pltpu.get_barrier_semaphore()
    others = [at_xy(cy, cx + d) for d in (1, 2, 3)] + [at_xy(cy + d, cx) for d in (1, 2, 3)]
    others += [at_z(cz + 1), at_z(cz - 1), sibling, following, previous, crossed]
    for other in others:
        pl.semaphore_signal(barrier, inc=1, device_id=other, device_id_type=MESH)

    sources = (q_hbm, k_hbm, v_hbm)

    def own_copy(n):
        return pltpu.make_async_copy(
            w_ref.at[:, pl.ds(n * CHUNK, CHUNK)], wbuf.at[n, cy * 2 + column], own_sem.at[n])

    def in_copy(index):
        return pltpu.make_async_copy(sources[index], inputs.at[index], in_sem.at[index])

    for n in range(CHUNKS):
        own_copy(n).start()
    for index in (1, 2, 0):
        in_copy(index).start()
    for n in range(CHUNKS):
        own_copy(n).wait()
    pl.semaphore_wait(barrier, len(others))

    def halo_copy(index):
        return pltpu.make_async_remote_copy(
            src_ref=sources[index].at[pl.ds(ROWS - HALO, HALO)], dst_ref=halo.at[index],
            send_sem=h_send.at[index], recv_sem=h_recv.at[index],
            device_id=following, device_id_type=MESH)

    for index in (1, 2, 0):
        halo_copy(index).start()

    def ring(kind, receiving):
        step = 1 if kind % 2 == 0 else -1
        if receiving:
            return step, (-step if kind < 2 else -2 * step)
        return step, (0 if kind < 2 else -step)

    def w_copy(n, number, receiving):
        if number < 4 or number >= 9:
            kind = number if number < 4 else (number - 9) % 4
            step, back = ring(kind, receiving)
            row = cy + back
            flip = number >= 13
            target = at_xy(cy + step, cx)
            low, high = (0, CUT) if number < 4 else (CUT, ROWS)
            middle = (low + high) // 2
            if kind == 2:
                high = middle
            if kind == 3:
                low = middle
        else:
            row = cy + (OFFS[number - 4] if number < 8 else 0)
            flip = receiving
            target = beside
            low, high = (0, CUT) if number < 8 else (CUT, ROWS)
        across = 1 - column if flip else column
        where = wbuf.at[n, mod(row) * 2 + across, pl.ds(low, high - low)]
        index = n * PER_CHUNK + number
        return pltpu.make_async_remote_copy(
            src_ref=where, dst_ref=where, send_sem=w_send.at[index], recv_sem=w_recv.at[index],
            device_id=target, device_id_type=MESH)

    def w_start(n, *numbers):
        for number in numbers:
            w_copy(n, number, False).start()

    def w_wait(n, *numbers):
        for number in numbers:
            w_copy(n, number, True).wait_recv()

    def w_own(n):
        w_start(n, 8, 0, 1, 9, 10, 4)

    def w_first(n):
        w_wait(n, 8)
        w_start(n, 13, 14)
        for kind in (0, 1):
            w_wait(n, kind)
            w_start(n, kind + 2, 5 + kind)
        for kind in (0, 1):
            w_wait(n, 9 + kind)
            w_start(n, 11 + kind)

    def w_second(n):
        w_wait(n, 2, 3)
        w_start(n, 7)
        for kind in (0, 1):
            w_wait(n, 13 + kind)
            w_start(n, 15 + kind)

    def w_third(n):
        w_wait(n, 4, 5, 6, 7, 11, 12, 15, 16)

    def a_copy(q, kind, receiving):
        low, size = 0, ROWS
        held = role
        if kind < 4:
            step, back = ring(kind, receiving)
            if kind >= 2:
                low, size = (ROWS // 2 if kind == 3 else 0), ROWS // 2
            target = at_z(cz + step)
        else:
            back = OFFS[kind - 4]
            held = 1 - role if receiving else role
            target = sibling
        where = abuf.at[held * SIDE + mod(cz + back), q, pl.ds(low, size)]
        index = q * 8 + kind
        return pltpu.make_async_remote_copy(
            src_ref=where, dst_ref=where, send_sem=a_send.at[index], recv_sem=a_recv.at[index],
            device_id=target, device_id_type=MESH)

    def p_copy(q):
        return pltpu.make_async_remote_copy(
            src_ref=abuf.at[2 * SIDE, q], dst_ref=abuf.at[SIDE + cz, q],
            send_sem=p_send.at[q], recv_sem=p_recv.at[q],
            device_id=crossed, device_id_type=MESH)

    def c_copy(n):
        return pltpu.make_async_remote_copy(
            src_ref=cout.at[n], dst_ref=cin.at[n], send_sem=c_send.at[n], recv_sem=c_recv.at[n],
            device_id=partner, device_id_type=MESH)

    def state_copy(part, stage, distance, receiving):
        held = (xstate, ystate)[stage]
        position = (cx, cy)[stage]
        index = mod(position - distance) if receiving else position
        target = at_xy(cy, cx + distance) if stage == 0 else at_xy(cy + distance, cx)
        number = part * 6 + stage * 3 + distance - 1
        where = held.at[part, index]
        return pltpu.make_async_remote_copy(
            src_ref=where, dst_ref=where,
            send_sem=s_send.at[number], recv_sem=s_recv.at[number],
            device_id=target, device_id_type=MESH)

    w_own(0)
    w_own(1)

    dec[...] = jnp.exp(-rates_ref[...])

    def lanes_of(tile):
        return pl.ds(pl.multiple_of(tile * LANES, LANES), LANES)

    def widen(index):
        in_copy(index).wait()

        def body(tile, carry):
            streams[index, tile, pl.ds(0, PAD), :] = jnp.zeros((PAD, LANES), F32)
            streams[index, tile, pl.ds(PAD, ROWS), :] = inputs[index, :, lanes_of(tile)].astype(F32)
            return carry

        lax.fori_loop(0, TILES, body, 0)

    def widen_halo(index):
        halo_copy(index).wait_recv()
        keep = jnp.where(ctx > 0, 1.0, 0.0).astype(F32)

        def body(tile, carry):
            rim = halo[index, :, lanes_of(tile)].astype(F32)
            streams[index, tile, pl.ds(0, PAD), :] = rim[HALO - PAD:] * keep
            return carry

        lax.fori_loop(0, TILES, body, 0)

    def spread(row):
        return jnp.broadcast_to(row, (SEGS, LANES))

    def strided(index, tile, start):
        return streams[index, tile, pl.ds(start, SEGS, stride=STEPS), :]

    def tap_rows(index, lanes):
        return [spread(taps_ref[index, pl.ds(j, 1), lanes]) for j in range(3)]

    def gate(k_taps, v_taps, k0, k1, k2, v0, v1, v2):
        kf = rounded(k_taps[0] * k0 + k_taps[1] * k1 + k_taps[2] * k2)
        vf = rounded(v_taps[0] * v0 + v_taps[1] * v1 + v_taps[2] * v2)
        return rounded(kf * vf)

    def first_tile(tile, carry):
        lanes = lanes_of(tile)
        decay = [spread(dec[pl.ds(r, 1), lanes]) for r in range(ORDER)]
        k_taps, v_taps = tap_rows(1, lanes), tap_rows(2, lanes)

        def step(i, held):
            k1, k2, v1, v2, states = held
            k0, v0 = strided(1, tile, PAD + i), strided(2, tile, PAD + i)
            gated = gate(k_taps, v_taps, k0, k1, k2, v0, v1, v2)
            gbuf[tile, i] = gated
            states = tuple(decay[r] * states[r] + gated for r in range(ORDER))
            return k0, k1, v0, v1, states

        zero = jnp.zeros((SEGS, LANES), F32)
        start = (strided(1, tile, PAD - 1), strided(1, tile, PAD - 2),
                 strided(2, tile, PAD - 1), strided(2, tile, PAD - 2), (zero,) * ORDER)
        states = lax.fori_loop(0, STEPS, step, start, unroll=4)[4]
        for r in range(ORDER):
            ends[tile, pl.ds(r, SEGS, stride=ORDER), :] = states[r]
        return carry

    def mend_tile(tile, carry):
        lanes = lanes_of(tile)
        k_taps, v_taps = tap_rows(1, lanes), tap_rows(2, lanes)
        k = [strided(1, tile, PAD + d) for d in (-2, -1, 0, 1)]
        v = [strided(2, tile, PAD + d) for d in (-2, -1, 0, 1)]
        changes = []
        for i in (0, 1):
            gated = gate(k_taps, v_taps, k[i + 2], k[i + 1], k[i], v[i + 2], v[i + 1], v[i])
            changes.append(gated - gbuf[tile, i])
            gbuf[tile, i] = gated
        rate = rates_ref[:, lanes]
        far, near = jnp.exp(-float(STEPS - 1) * rate), jnp.exp(-float(STEPS - 2) * rate)
        for r in range(ORDER):
            rows = pl.ds(r, SEGS, stride=ORDER)
            ends[tile, rows, :] = (ends[tile, rows, :] + spread(far[r:r + 1]) * changes[0]
                                   + spread(near[r:r + 1]) * changes[1])
        return carry

    def combine_tile(part):
        def body(tile, carry):
            jump = jnp.exp(-float(STEPS) * rates_ref[:, lanes_of(tile)])
            state = jnp.zeros((ORDER, LANES), F32)
            for seg in range(SEGS):
                inits[tile, pl.ds(seg * ORDER, ORDER), :] = state
                state = jump * state + ends[tile, pl.ds(seg * ORDER, ORDER), :]
            xstate[part, cx, :, lanes_of(tile - part * (TILES // PARTS))] = state
            return carry
        return body

    def row_tile(part):
        def body(tile, carry):
            lanes = lanes_of(tile - part * (TILES // PARTS))
            jump = jnp.exp(-float(ROWS) * rates_ref[:, lanes_of(tile)])
            state = jnp.zeros((ORDER, LANES), F32)
            for position in range(SIDE):
                state = jump * state + xstate[part, position, :, lanes]
            ystate[part, cy, :, lanes] = state
            return carry
        return body

    def seed_tile(part):
        def body(tile, carry):
            lanes = lanes_of(tile - part * (TILES // PARTS))
            rate = rates_ref[:, lanes_of(tile)]
            jump_x = jnp.exp(-float(ROWS) * rate)
            jump_y = jnp.exp(-float(ROWS * SIDE) * rate)
            before_x = jnp.zeros((ORDER, LANES), F32)
            before_y = jnp.zeros((ORDER, LANES), F32)
            for position in range(SIDE - 1):
                before_x = jnp.where(
                    position < cx, jump_x * before_x + xstate[part, position, :, lanes], before_x)
                before_y = jnp.where(
                    position < cy, jump_y * before_y + ystate[part, position, :, lanes], before_y)
            shift = (cx * ROWS).astype(F32)
            state = before_x + jnp.exp(-shift * rate) * before_y
            jump = jnp.exp(-float(STEPS) * rate)
            for seg in range(SEGS):
                rows = pl.ds(seg * ORDER, ORDER)
                inits[tile, rows, :] = inits[tile, rows, :] + state
                state = jump * state
            return carry
        return body

    target_block = jnp.where(role == 0, cz, 2 * SIDE)

    def second_tile(part):
        def body(tile, carry):
            lanes = lanes_of(tile)
            decay = [spread(dec[pl.ds(r, 1), lanes]) for r in range(ORDER)]
            weight = [spread(res_ref[pl.ds(r, 1), lanes]) for r in range(ORDER)]
            q_taps = tap_rows(0, lanes)

            def step(i, held):
                q1, q2, states = held
                q0 = strided(0, tile, PAD + i)
                qf = rounded(q_taps[0] * q0 + q_taps[1] * q1 + q_taps[2] * q2)
                gated = gbuf[tile, i]
                states = tuple(decay[r] * states[r] + gated for r in range(ORDER))
                terms = [weight[r] * states[r] for r in range(ORDER)]
                while len(terms) > 1:
                    terms = [terms[j] + terms[j + 1] for j in range(0, len(terms), 2)]
                ybuf[pl.ds(i, SEGS, stride=STEPS), :] = qf * terms[0]
                return q0, q1, states

            start = (strided(0, tile, PAD - 1), strided(0, tile, PAD - 2),
                     tuple(inits[tile, pl.ds(r, SEGS, stride=ORDER), :] for r in range(ORDER)))
            lax.fori_loop(0, STEPS, step, start, unroll=4)
            abuf[target_block, part, :, lanes_of(tile - part * (TILES // PARTS))] = (
                ybuf[...].astype(BF16))
            return carry
        return body

    def tiles(part, body):
        each = TILES // PARTS
        lax.fori_loop(part * each, (part + 1) * each, body, 0)

    def states_out(part, stage):
        for distance in (1, 3, 2):
            state_copy(part, stage, distance, False).start()

    def states_in(part, stage):
        for distance in (1, 3, 2):
            state_copy(part, stage, distance, True).wait_recv()

    def a_begin(q):
        @pl.when(role == 0)
        def _():
            for kind in (0, 1, 4):
                a_copy(q, kind, False).start()

        @pl.when(role == 1)
        def _():
            p_copy(q).start()

    def a_cross(q):
        @pl.when(role == 1)
        def _():
            p_copy(q).wait_recv()
            for kind in (0, 1, 4):
                a_copy(q, kind, False).start()

    def a_middle(q):
        for kind in (0, 1):
            a_copy(q, kind, True).wait_recv()
            a_copy(q, kind + 2, False).start()
            a_copy(q, kind + 5, False).start()

    def a_end(q):
        for kind in (2, 3):
            a_copy(q, kind, True).wait_recv()
        a_copy(q, 7, False).start()

    def a_sibling(q, *kinds):
        for kind in kinds:
            a_copy(q, kind, True).wait_recv()

    def multiply(group, z, q, n):
        block = mod(z)
        acc[group, n] += jnp.dot(
            abuf[group * SIDE + block, q], wbuf[n, block * 2 + q], preferred_element_type=F32)

    def sweep(groups, offsets, parts, chunks):
        g0, gn = groups
        o0, on = offsets
        q0, qn = parts
        n0, nn = chunks

        def body(t, carry):
            n = n0 + t // (gn * on * qn)
            rest = t % (gn * on * qn)
            multiply(g0 + rest // (on * qn), cz + o0 + rest % on, q0 + (rest // on) % qn, n)
            return carry

        lax.fori_loop(0, gn * on * qn * nn, body, 0)

    def c_begin(n):
        cout[n] = acc[1, n].astype(BF16)
        c_copy(n).start()

    def c_end(n):
        c_copy(n).wait_recv()
        out_ref[:, pl.ds(n * CHUNK, CHUNK)] = (acc[0, n] + cin[n].astype(F32)).astype(BF16)

    NEAR, FAR, EVERY = (-1, 3), (2, 1), (-1, 4)
    BOTH, OWN, THEIRS = (0, 2), (0, 1), (1, 1)

    widen(1)
    widen(2)
    tiles(0, first_tile)
    widen_halo(1)
    widen_halo(2)
    tiles(0, mend_tile)
    tiles(0, combine_tile(0))
    states_out(0, 0)
    tiles(1, first_tile)
    tiles(1, mend_tile)
    tiles(1, combine_tile(1))
    states_out(1, 0)
    w_first(0)
    w_own(2)
    states_in(0, 0)
    tiles(0, row_tile(0))
    states_out(0, 1)
    widen(0)
    widen_halo(0)
    states_in(1, 0)
    tiles(1, row_tile(1))
    states_out(1, 1)
    w_second(0)
    states_in(0, 1)
    tiles(0, seed_tile(0))
    tiles(0, second_tile(0))
    a_begin(0)
    w_first(1)
    w_own(3)
    states_in(1, 1)
    tiles(1, seed_tile(1))
    tiles(1, second_tile(1))
    a_begin(1)
    w_second(1)
    w_third(0)
    acc[...] = jnp.zeros_like(acc)
    a_cross(0)
    w_first(2)
    a_cross(1)
    a_middle(0)
    w_second(2)
    w_third(1)
    a_middle(1)
    w_first(3)
    a_end(0)
    a_sibling(0, 4, 5, 6)
    sweep(BOTH, NEAR, (0, 1), (0, 2))
    w_third(2)
    w_second(3)
    a_end(1)
    a_sibling(1, 4, 5, 6)
    sweep(BOTH, NEAR, (1, 1), (0, 2))
    a_sibling(0, 7)
    a_sibling(1, 7)
    sweep(THEIRS, FAR, (0, 2), (0, 1))
    c_begin(0)
    sweep(THEIRS, FAR, (0, 2), (1, 1))
    c_begin(1)
    sweep(THEIRS, EVERY, (0, 2), (2, 1))
    c_begin(2)
    sweep(OWN, FAR, (0, 2), (0, 2))
    sweep(OWN, EVERY, (0, 2), (2, 1))
    w_third(3)
    sweep(THEIRS, EVERY, (0, 2), (3, 1))
    c_begin(3)
    sweep(OWN, EVERY, (0, 2), (3, 1))
    for n in range(CHUNKS):
        c_end(n)

    for n in range(CHUNKS):
        for number in range(PER_CHUNK):
            w_copy(n, number, False).wait_send()
        c_copy(n).wait_send()
    for q in range(PARTS):
        for kind in range(8):
            a_copy(q, kind, False).wait_send()
        for stage in range(2):
            for distance in (1, 2, 3):
                state_copy(q, stage, distance, False).wait_send()

    @pl.when(role == 1)
    def _():
        for q in range(PARTS):
            p_copy(q).wait_send()

    for index in range(3):
        halo_copy(index).wait_send()


def per_device(query, keys_in, values_in, short_taps, mode_rates, mode_residues, out_weight):
    vmem = pl.BlockSpec(memory_space=pltpu.VMEM)
    hbm = pl.BlockSpec(memory_space=pl.ANY)
    dma = pltpu.SemaphoreType.DMA
    return pl.pallas_call(
        kernel,
        out_shape=jax.ShapeDtypeStruct((ROWS, WIDTH), BF16),
        in_specs=[hbm] * 3 + [vmem] * 3 + [hbm],
        out_specs=vmem,
        scratch_shapes=[
            pltpu.VMEM((CHUNKS, 2 * SIDE, ROWS, CHUNK), BF16),
            pltpu.VMEM((2 * SIDE + 1, PARTS, ROWS, PART), BF16),
            pltpu.VMEM((2, CHUNKS, ROWS, CHUNK), F32),
            pltpu.VMEM((CHUNKS, ROWS, CHUNK), BF16),
            pltpu.VMEM((CHUNKS, ROWS, CHUNK), BF16),
            pltpu.VMEM((3, ROWS, WIDTH), BF16),
            pltpu.VMEM((3, TILES, PAD + ROWS, LANES), F32),
            pltpu.VMEM((TILES, STEPS, SEGS, LANES), F32),
            pltpu.VMEM((ROWS, LANES), F32),
            pltpu.VMEM((3, HALO, WIDTH), BF16),
            pltpu.VMEM((ORDER, WIDTH), F32),
            pltpu.VMEM((TILES, SEGS * ORDER, LANES), F32),
            pltpu.VMEM((TILES, SEGS * ORDER, LANES), F32),
            pltpu.VMEM((PARTS, SIDE, ORDER, PART), F32),
            pltpu.VMEM((PARTS, SIDE, ORDER, PART), F32),
            dma((CHUNKS * PER_CHUNK,)), dma((CHUNKS * PER_CHUNK,)),
            dma((PARTS * 8,)), dma((PARTS * 8,)), dma((PARTS,)), dma((PARTS,)),
            dma((CHUNKS,)), dma((CHUNKS,)), dma((3,)), dma((3,)),
            dma((PARTS * 6,)), dma((PARTS * 6,)), dma((CHUNKS,)), dma((3,)),
        ],
        compiler_params=pltpu.CompilerParams(
            collective_id=0, has_side_effects=True, vmem_limit_bytes=56 * 1024 * 1024),
        cost_estimate=pl.CostEstimate(
            flops=2 * ROWS * 8192 * WIDTH, bytes_accessed=6 * 1024 * 1024, transcendentals=0),
    )(query, keys_in, values_in, short_taps, mode_rates, mode_residues, out_weight)


def solution(mesh):
    in_specs = (
        P("ctx", "ch"),
        P("ctx", "ch"),
        P("ctx", "ch"),
        P(None, None, "ch"),
        P(None, "ch"),
        P(None, "ch"),
        P("ctx", "ch"),
    )
    return jax.shard_map(
        per_device, mesh=mesh, in_specs=in_specs, out_specs=P("ctx", "ch"), check_vma=False
    )
```

time: 304 us -> 112 us (0.37)
  waiting for transfers between devices: 165 us -> 0 us
  Pallas kernels: 0 us -> 109 us
  matrix products: 54.5 us -> 0 us
  starting transfers between devices: 23.6 us -> 0 us
  blocking collectives: 20.6 us -> 0 us
  local copies, waits for them, and re-layouts: 17.6 us -> 2.26 us
  between operations: 13.9 us -> 0.01 us
  other arithmetic: 8.07 us -> 0 us
    all_gather x2 -> x0, waiting for transfers between devices: 165 us -> none  [the longest x1 113 us: per_device(): piece = lax.all_gather(out_weight, 'ctx', axis=0, tiled=True)]
    pallas_call x0 -> x1, Pallas kernels: none -> 109 us  [per_device(): pl.pallas_call(kernel, out_shape=jax.ShapeDtypeStruct((ROWS, WIDTH), BF16...]
    dot_general x5 -> x0, matrix products: 49.9 us -> none  [the longest x1 16.8 us: modal_conv(): jnp.einsum('irc,jrc->cij', powers * residues[None], lifted, precision=HIG...]
    all_to_all x1 -> x0, blocking collectives: 20.6 us -> none  [per_device(): lax.all_to_all(result_channel, 'ctx', split_axis=0, concat_axis=1, tiled=...]
    all_to_all x2 -> x0, starting transfers between devices: 13.2 us -> none  [the longest x1 6.73 us: per_device(): lax.all_to_all(query_feat, 'ctx', split_axis=1, concat_axis=0, tiled=True)]
    ppermute x3 -> x0, starting transfers between devices: 9.85 us -> none  [passed_along(): lax.ppermute(value, axis, [(source, source + steps) for source in range(f...]
    convert_element_type x8 -> x0, local copies, waits for them, and re-layouts: 4.67 us -> none  [the longest x4 2.34 us: featurize(): return depthwise(padded, short_taps[index]).astype(jnp.bfloat16)]
    conv_general_dilated x3 -> x0, matrix products: 4.66 us -> none  [depthwise(): lax.conv_general_dilated(padded[None], kernel, (1,), 'VALID', dimension_n...]
  transfers between devices with their start and end apart: 7 -> 0, of which waited for: 2 -> 0; matrix products, arithmetic and copies ran while one was open for 20% -> 0% of each run, Pallas kernels for 0% -> 0%
where the time goes in v2:
time: 112 us; the launch traced here: 111 us
  Pallas kernels  109 us (97%)
  local copies, waits for them, and re-layouts  2.26 us (2%)
    pallas_call x1, Pallas kernels, per_device(): pl.pallas_call(kernel, out_shape=jax.ShapeDtypeStruct((ROWS, WIDTH), BF16...  109 us
    unnamed x1, local copies, waits for them, and re-layouts  2.26 us

profile of v2, /device:TPU:1, one launch (start us, length us, event | category | flops | bytes accessed | tf_op | source)
XLA Modules:
  0.0 111.3 jit_solution(5226792074792352577)
XLA Ops:
  0.0 109.1 %shard_map.73 = bf16[512,1024]{1,0:T(8,128)(2,1)} custom-call(bf16[512,1024]{1,0:T(8,128)(2,1)} %q_hbm.1, bf16[512,1024]{1,0:T(8,128)(2,1)} %k_hbm.1, bf16[512,1024]{1,0:T(8,128)(2,1)} %v_hbm.1, f32[3,3,1024]{2,1,0:T(4,128)} %taps_ref.1, f32[16,1024]{1,0:T(8,128)} %rates_ref.1, f32[16,1024]{1,0:T(8,128)} %res_ref.1, bf16[512,1024]{1,0:T(8,128)(2,1)} %w_ref.1), custom_call_target="tpu_custom_call" | custom-call | flops 8589934592 | bytes 6291456 | tf_op jit(solution)/shard_map/pallas_call | solution.py:521
  109.1 2.3 %copy.9 = bf16[512,1024]{1,0:T(8,128)(2,1)} copy(bf16[512,1024]{1,0:T(8,128)(2,1)} %shard_map.73) | data formatting | bytes 2097152

commit v3 on v2

--- a/solution.py
+++ b/solution.py
@@ -18,17 +18,16 @@
 HALO = 16
 PARTS = 2
 PART = WIDTH // PARTS
+PIECES = 4
+PIECE = WIDTH // PIECES
 CHUNKS = 4
 CHUNK = WIDTH // CHUNKS
 CUT = 224
 OFFS = (0, -1, 1, 2)
-PER_CHUNK = 17
+PER_GROUP = 17
+GROUPS = ((0, 1), (1, 2), (3, 1))
 F32 = jnp.float32
 BF16 = jnp.bfloat16
-
-
-def rounded(value):
-    return value.astype(BF16).astype(F32)
 
 
 def kernel(
@@ -70,7 +69,7 @@
 
     def own_copy(n):
         return pltpu.make_async_copy(
-            w_ref.at[:, pl.ds(n * CHUNK, CHUNK)], wbuf.at[n, cy * 2 + column], own_sem.at[n])
+            w_ref.at[:, pl.ds(n * CHUNK, CHUNK)], wbuf.at[cy * 2 + column, n], own_sem.at[n])
 
     def in_copy(index):
         return pltpu.make_async_copy(sources[index], inputs.at[index], in_sem.at[index])
@@ -79,18 +78,18 @@
         own_copy(n).start()
     for index in (1, 2, 0):
         in_copy(index).start()
-    for n in range(CHUNKS):
-        own_copy(n).wait()
-    pl.semaphore_wait(barrier, len(others))
-
     def halo_copy(index):
         return pltpu.make_async_remote_copy(
             src_ref=sources[index].at[pl.ds(ROWS - HALO, HALO)], dst_ref=halo.at[index],
             send_sem=h_send.at[index], recv_sem=h_recv.at[index],
             device_id=following, device_id_type=MESH)
 
-    for index in (1, 2, 0):
-        halo_copy(index).start()
+    def enter():
+        pl.semaphore_wait(barrier, len(others))
+        for index in (1, 2, 0):
+            halo_copy(index).start()
+        for n in range(CHUNKS):
+            own_copy(n).wait()
 
     def ring(kind, receiving):
         step = 1 if kind % 2 == 0 else -1
@@ -117,8 +116,8 @@
             target = beside
             low, high = (0, CUT) if number < 8 else (CUT, ROWS)
         across = 1 - column if flip else column
-        where = wbuf.at[n, mod(row) * 2 + across, pl.ds(low, high - low)]
-        index = n * PER_CHUNK + number
+        where = wbuf.at[mod(row) * 2 + across, pl.ds(*GROUPS[n]), pl.ds(low, high - low)]
+        index = n * PER_GROUP + number
         return pltpu.make_async_remote_copy(
             src_ref=where, dst_ref=where, send_sem=w_send.at[index], recv_sem=w_recv.at[index],
             device_id=target, device_id_type=MESH)
@@ -195,8 +194,6 @@
             send_sem=s_send.at[number], recv_sem=s_recv.at[number],
             device_id=target, device_id_type=MESH)
 
-    w_own(0)
-    w_own(1)
 
     dec[...] = jnp.exp(-rates_ref[...])
 
@@ -234,9 +231,9 @@
         return [spread(taps_ref[index, pl.ds(j, 1), lanes]) for j in range(3)]
 
     def gate(k_taps, v_taps, k0, k1, k2, v0, v1, v2):
-        kf = rounded(k_taps[0] * k0 + k_taps[1] * k1 + k_taps[2] * k2)
-        vf = rounded(v_taps[0] * v0 + v_taps[1] * v1 + v_taps[2] * v2)
-        return rounded(kf * vf)
+        kf = k_taps[0] * k0 + k_taps[1] * k1 + k_taps[2] * k2
+        vf = v_taps[0] * v0 + v_taps[1] * v1 + v_taps[2] * v2
+        return kf * vf
 
     def first_tile(tile, carry):
         lanes = lanes_of(tile)
@@ -324,37 +321,37 @@
 
     target_block = jnp.where(role == 0, cz, 2 * SIDE)
 
-    def second_tile(part):
-        def body(tile, carry):
-            lanes = lanes_of(tile)
-            decay = [spread(dec[pl.ds(r, 1), lanes]) for r in range(ORDER)]
-            weight = [spread(res_ref[pl.ds(r, 1), lanes]) for r in range(ORDER)]
-            q_taps = tap_rows(0, lanes)
-
-            def step(i, held):
-                q1, q2, states = held
-                q0 = strided(0, tile, PAD + i)
-                qf = rounded(q_taps[0] * q0 + q_taps[1] * q1 + q_taps[2] * q2)
-                gated = gbuf[tile, i]
-                states = tuple(decay[r] * states[r] + gated for r in range(ORDER))
-                terms = [weight[r] * states[r] for r in range(ORDER)]
-                while len(terms) > 1:
-                    terms = [terms[j] + terms[j + 1] for j in range(0, len(terms), 2)]
-                ybuf[pl.ds(i, SEGS, stride=STEPS), :] = qf * terms[0]
-                return q0, q1, states
-
-            start = (strided(0, tile, PAD - 1), strided(0, tile, PAD - 2),
-                     tuple(inits[tile, pl.ds(r, SEGS, stride=ORDER), :] for r in range(ORDER)))
-            lax.fori_loop(0, STEPS, step, start, unroll=4)
-            abuf[target_block, part, :, lanes_of(tile - part * (TILES // PARTS))] = (
-                ybuf[...].astype(BF16))
-            return carry
-        return body
+    def second_tile(tile, carry):
+        lanes = lanes_of(tile)
+        decay = [spread(dec[pl.ds(r, 1), lanes]) for r in range(ORDER)]
+        weight = [spread(res_ref[pl.ds(r, 1), lanes]) for r in range(ORDER)]
+        q_taps = tap_rows(0, lanes)
+
+        def step(i, held):
+            q1, q2, states = held
+            q0 = strided(0, tile, PAD + i)
+            qf = q_taps[0] * q0 + q_taps[1] * q1 + q_taps[2] * q2
+            gated = gbuf[tile, i]
+            states = tuple(decay[r] * states[r] + gated for r in range(ORDER))
+            terms = [weight[r] * states[r] for r in range(ORDER)]
+            while len(terms) > 1:
+                terms = [terms[j] + terms[j + 1] for j in range(0, len(terms), 2)]
+            ybuf[pl.ds(i, SEGS, stride=STEPS), :] = qf * terms[0]
+            return q0, q1, states
+
+        start = (strided(0, tile, PAD - 1), strided(0, tile, PAD - 2),
+                 tuple(inits[tile, pl.ds(r, SEGS, stride=ORDER), :] for r in range(ORDER)))
+        lax.fori_loop(0, STEPS, step, start, unroll=4)
+        abuf[target_block, tile // 2, :, lanes_of(tile % 2)] = ybuf[...].astype(BF16)
+        return carry
 
     def tiles(part, body):
         each = TILES // PARTS
         lax.fori_loop(part * each, (part + 1) * each, body, 0)
 
+    def outputs(q):
+        lax.fori_loop(2 * q, 2 * q + 2, second_tile, 0)
+
     def states_out(part, stage):
         for distance in (1, 3, 2):
             state_copy(part, stage, distance, False).start()
@@ -363,22 +360,21 @@
         for distance in (1, 3, 2):
             state_copy(part, stage, distance, True).wait_recv()
 
-    def a_begin(q):
-        @pl.when(role == 0)
+    def when(wanted, call, *args):
+        @pl.when(role == wanted)
         def _():
-            for kind in (0, 1, 4):
-                a_copy(q, kind, False).start()
-
-        @pl.when(role == 1)
-        def _():
-            p_copy(q).start()
+            call(*args)
+
+    def a_start(q, *kinds):
+        for kind in kinds:
+            a_copy(q, kind, False).start()
+
+    def p_begin(q):
+        p_copy(q).start()
 
     def a_cross(q):
-        @pl.when(role == 1)
-        def _():
-            p_copy(q).wait_recv()
-            for kind in (0, 1, 4):
-                a_copy(q, kind, False).start()
+        p_copy(q).wait_recv()
+        a_start(q, 0, 1, 4)
 
     def a_middle(q):
         for kind in (0, 1):
@@ -395,10 +391,17 @@
         for kind in kinds:
             a_copy(q, kind, True).wait_recv()
 
+    def a_pair(q):
+        a_sibling(q, 4, 5, 6, 7)
+
     def multiply(group, z, q, n):
         block = mod(z)
-        acc[group, n] += jnp.dot(
-            abuf[group * SIDE + block, q], wbuf[n, block * 2 + q], preferred_element_type=F32)
+        total = acc[group, n]
+        for s in range(2):
+            total += jnp.dot(
+                abuf[group * SIDE + block, 2 * q + s], wbuf[block * 2 + q, n, pl.ds(s * PIECE, PIECE)],
+                preferred_element_type=F32)
+        acc[group, n] = total
 
     def sweep(groups, offsets, parts, chunks):
         g0, gn = groups
@@ -427,6 +430,9 @@
 
     widen(1)
     widen(2)
+    widen(0)
+    enter()
+    w_start(0, 8, 0, 1, 9, 10)
     tiles(0, first_tile)
     widen_halo(1)
     widen_halo(2)
@@ -437,77 +443,103 @@
     tiles(1, mend_tile)
     tiles(1, combine_tile(1))
     states_out(1, 0)
-    w_first(0)
-    w_own(2)
+    widen_halo(0)
     states_in(0, 0)
     tiles(0, row_tile(0))
     states_out(0, 1)
-    widen(0)
-    widen_halo(0)
     states_in(1, 0)
     tiles(1, row_tile(1))
     states_out(1, 1)
-    w_second(0)
+    w_start(0, 4)
+    w_start(1, 8, 4)
     states_in(0, 1)
     tiles(0, seed_tile(0))
-    tiles(0, second_tile(0))
-    a_begin(0)
+    outputs(0)
+    when(1, p_begin, 0)
+    when(0, a_start, 0, 0, 1, 4)
+    outputs(1)
+    when(1, p_begin, 1)
+    when(0, a_start, 1, 0, 1, 4)
+    states_in(1, 1)
+    w_first(0)
+    w_start(1, 0, 1, 9, 10)
+    w_own(2)
+    tiles(1, seed_tile(1))
+    outputs(2)
+    when(1, p_begin, 2)
+    when(0, a_start, 2, 4)
+    when(1, a_cross, 0)
+    outputs(3)
+    when(1, p_begin, 3)
+    when(0, a_start, 3, 4)
+    when(1, a_cross, 1)
+    acc[...] = jnp.zeros_like(acc)
+    when(1, a_middle, 0)
+    w_second(0)
+    when(1, a_cross, 2)
+    when(1, a_middle, 1)
+    when(1, a_cross, 3)
+    when(1, a_end, 0)
+    when(1, a_middle, 2)
+    when(1, a_end, 1)
+    when(1, a_middle, 3)
+    when(0, a_middle, 0)
+    when(0, a_middle, 1)
+    when(0, a_start, 2, 0, 1)
+    when(0, a_start, 3, 0, 1)
     w_first(1)
-    w_own(3)
-    states_in(1, 1)
-    tiles(1, seed_tile(1))
-    tiles(1, second_tile(1))
-    a_begin(1)
+    when(1, a_end, 2)
+    when(1, a_end, 3)
+    w_third(0)
+    when(0, a_pair, 0)
+    when(0, a_pair, 1)
+    sweep(THEIRS, EVERY, (0, 1), (0, 1))
+    when(0, a_pair, 2)
+    when(0, a_pair, 3)
+    sweep(THEIRS, EVERY, (1, 1), (0, 1))
+    c_begin(0)
     w_second(1)
-    w_third(0)
-    acc[...] = jnp.zeros_like(acc)
-    a_cross(0)
+    when(0, a_middle, 2)
+    when(0, a_end, 0)
+    when(0, a_middle, 3)
+    when(0, a_end, 1)
     w_first(2)
-    a_cross(1)
-    a_middle(0)
-    w_second(2)
     w_third(1)
-    a_middle(1)
-    w_first(3)
-    a_end(0)
-    a_sibling(0, 4, 5, 6)
-    sweep(BOTH, NEAR, (0, 1), (0, 2))
-    w_third(2)
-    w_second(3)
-    a_end(1)
-    a_sibling(1, 4, 5, 6)
-    sweep(BOTH, NEAR, (1, 1), (0, 2))
-    a_sibling(0, 7)
-    a_sibling(1, 7)
-    sweep(THEIRS, FAR, (0, 2), (0, 1))
-    c_begin(0)
-    sweep(THEIRS, FAR, (0, 2), (1, 1))
+    sweep(THEIRS, EVERY, (0, 2), (1, 1))
     c_begin(1)
     sweep(THEIRS, EVERY, (0, 2), (2, 1))
     c_begin(2)
-    sweep(OWN, FAR, (0, 2), (0, 2))
-    sweep(OWN, EVERY, (0, 2), (2, 1))
-    w_third(3)
+    when(0, a_end, 2)
+    when(0, a_end, 3)
+    w_second(2)
+    when(1, a_pair, 0)
+    when(1, a_pair, 1)
+    when(1, a_pair, 2)
+    when(1, a_pair, 3)
+    sweep(OWN, EVERY, (0, 2), (0, 3))
+    w_third(2)
     sweep(THEIRS, EVERY, (0, 2), (3, 1))
     c_begin(3)
     sweep(OWN, EVERY, (0, 2), (3, 1))
     for n in range(CHUNKS):
         c_end(n)
 
+    for n in range(len(GROUPS)):
+        for number in range(PER_GROUP):
+            w_copy(n, number, False).wait_send()
     for n in range(CHUNKS):
-        for number in range(PER_CHUNK):
-            w_copy(n, number, False).wait_send()
         c_copy(n).wait_send()
-    for q in range(PARTS):
+    for q in range(PIECES):
         for kind in range(8):
             a_copy(q, kind, False).wait_send()
+    for q in range(PARTS):
         for stage in range(2):
             for distance in (1, 2, 3):
                 state_copy(q, stage, distance, False).wait_send()
 
     @pl.when(role == 1)
     def _():
-        for q in range(PARTS):
+        for q in range(PIECES):
             p_copy(q).wait_send()
 
     for index in range(3):
@@ -524,8 +556,8 @@
         in_specs=[hbm] * 3 + [vmem] * 3 + [hbm],
         out_specs=vmem,
         scratch_shapes=[
-            pltpu.VMEM((CHUNKS, 2 * SIDE, ROWS, CHUNK), BF16),
-            pltpu.VMEM((2 * SIDE + 1, PARTS, ROWS, PART), BF16),
+            pltpu.VMEM((2 * SIDE, CHUNKS, ROWS, CHUNK), BF16),
+            pltpu.VMEM((2 * SIDE + 1, PIECES, ROWS, PIECE), BF16),
             pltpu.VMEM((2, CHUNKS, ROWS, CHUNK), F32),
             pltpu.VMEM((CHUNKS, ROWS, CHUNK), BF16),
             pltpu.VMEM((CHUNKS, ROWS, CHUNK), BF16),
@@ -539,8 +571,8 @@
             pltpu.VMEM((TILES, SEGS * ORDER, LANES), F32),
             pltpu.VMEM((PARTS, SIDE, ORDER, PART), F32),
             pltpu.VMEM((PARTS, SIDE, ORDER, PART), F32),
-            dma((CHUNKS * PER_CHUNK,)), dma((CHUNKS * PER_CHUNK,)),
-            dma((PARTS * 8,)), dma((PARTS * 8,)), dma((PARTS,)), dma((PARTS,)),
+            dma((len(GROUPS) * PER_GROUP,)), dma((len(GROUPS) * PER_GROUP,)),
+            dma((PIECES * 8,)), dma((PIECES * 8,)), dma((PIECES,)), dma((PIECES,)),
             dma((CHUNKS,)), dma((CHUNKS,)), dma((3,)), dma((3,)),
             dma((PARTS * 6,)), dma((PARTS * 6,)), dma((CHUNKS,)), dma((3,)),
         ],

time: 112 us -> 95.5 us (0.85)
  Pallas kernels: 109 us -> 91.6 us
    pallas_call x1, Pallas kernels: 109 us -> 91.6 us  [per_device(): pl.pallas_call(kernel, out_shape=jax.ShapeDtypeStruct((ROWS, WIDTH), BF16...]
where the time goes in v3:
time: 95.5 us; the launch traced here: 93.9 us
  Pallas kernels  91.6 us (96%)
  local copies, waits for them, and re-layouts  2.26 us (2%)
    pallas_call x1, Pallas kernels, per_device(): pl.pallas_call(kernel, out_shape=jax.ShapeDtypeStruct((ROWS, WIDTH), BF16...  91.6 us
    unnamed x1, local copies, waits for them, and re-layouts  2.26 us

profile of v3, /device:TPU:1, one launch (start us, length us, event | category | flops | bytes accessed | tf_op | source)
XLA Modules:
  0.0 93.9 jit_solution(3253740294831454823)
XLA Ops:
  0.0 91.6 %shard_map.73 = bf16[512,1024]{1,0:T(8,128)(2,1)} custom-call(bf16[512,1024]{1,0:T(8,128)(2,1)} %q_hbm.1, bf16[512,1024]{1,0:T(8,128)(2,1)} %k_hbm.1, bf16[512,1024]{1,0:T(8,128)(2,1)} %v_hbm.1, f32[3,3,1024]{2,1,0:T(4,128)} %taps_ref.1, f32[16,1024]{1,0:T(8,128)} %rates_ref.1, f32[16,1024]{1,0:T(8,128)} %res_ref.1, bf16[512,1024]{1,0:T(8,128)(2,1)} %w_ref.1), custom_call_target="tpu_custom_call" | custom-call | flops 8589934592 | bytes 6291456 | tf_op jit(solution)/shard_map/pallas_call | solution.py:553
  91.7 2.3 %copy.9 = bf16[512,1024]{1,0:T(8,128)(2,1)} copy(bf16[512,1024]{1,0:T(8,128)(2,1)} %shard_map.73) | data formatting | bytes 2097152

commit v4 on v3

--- a/solution.py
+++ b/solution.py
@@ -25,14 +25,14 @@
 CUT = 224
 OFFS = (0, -1, 1, 2)
 PER_GROUP = 17
-GROUPS = ((0, 1), (1, 2), (3, 1))
+GROUPS = ((0, 2), (2, 1), (3, 1))
 F32 = jnp.float32
 BF16 = jnp.bfloat16
 
 
 def kernel(
     q_hbm, k_hbm, v_hbm, taps_ref, rates_ref, res_ref, w_ref, out_ref,
-    wbuf, abuf, acc, cout, cin, inputs, streams, gbuf, ybuf, halo, dec, ends, inits, xstate, ystate,
+    wbuf, abuf, acc, early, cout, cin, inputs, streams, gbuf, ybuf, halo, dec, ends, inits, xstate, ystate,
     w_send, w_recv, a_send, a_recv, p_send, p_recv, c_send, c_recv, h_send, h_recv, s_send, s_recv,
     own_sem, in_sem,
 ):
@@ -394,45 +394,47 @@
     def a_pair(q):
         a_sibling(q, 4, 5, 6, 7)
 
-    def multiply(group, z, q, n):
-        block = mod(z)
-        total = acc[group, n]
-        for s in range(2):
-            total += jnp.dot(
-                abuf[group * SIDE + block, 2 * q + s], wbuf[block * 2 + q, n, pl.ds(s * PIECE, PIECE)],
-                preferred_element_type=F32)
-        acc[group, n] = total
-
-    def sweep(groups, offsets, parts, chunks):
-        g0, gn = groups
-        o0, on = offsets
-        q0, qn = parts
-        n0, nn = chunks
-
-        def body(t, carry):
-            n = n0 + t // (gn * on * qn)
-            rest = t % (gn * on * qn)
-            multiply(g0 + rest // (on * qn), cz + o0 + rest % on, q0 + (rest // on) % qn, n)
+    def product(group, n):
+        left = jnp.concatenate(
+            [abuf[group * SIDE + block, q] for block in range(SIDE) for q in range(PIECES)], 1)
+        right = jnp.concatenate([wbuf[j, n] for j in range(2 * SIDE)], 0)
+        return jnp.dot(left, right, preferred_element_type=F32)
+
+    def nearby(centre, n, offsets):
+        blocks = [mod(centre + offset) for offset in offsets]
+        left = jnp.concatenate(
+            [abuf[SIDE + block, q] for block in blocks for q in range(PIECES)], 1)
+        right = jnp.concatenate([wbuf[block * 2 + j, n] for block in blocks for j in range(2)], 0)
+        return jnp.dot(left, right, preferred_element_type=F32)
+
+    def partial(n):
+        cout[n] = product(1, n).astype(BF16)
+
+    def prepare(centre, n):
+        early[n] = nearby(centre, n, OFFS[:3])
+
+    def finish(centre, n):
+        cout[n] = (early[n] + nearby(centre, n, OFFS[3:])).astype(BF16)
+
+    def own(first, count):
+        def body(n, carry):
+            acc[n] = product(0, n)
             return carry
 
-        lax.fori_loop(0, gn * on * qn * nn, body, 0)
+        lax.fori_loop(first, first + count, body, 0)
 
     def c_begin(n):
-        cout[n] = acc[1, n].astype(BF16)
         c_copy(n).start()
 
     def c_end(n):
         c_copy(n).wait_recv()
-        out_ref[:, pl.ds(n * CHUNK, CHUNK)] = (acc[0, n] + cin[n].astype(F32)).astype(BF16)
-
-    NEAR, FAR, EVERY = (-1, 3), (2, 1), (-1, 4)
-    BOTH, OWN, THEIRS = (0, 2), (0, 1), (1, 1)
+        out_ref[:, pl.ds(n * CHUNK, CHUNK)] = (acc[n] + cin[n].astype(F32)).astype(BF16)
 
     widen(1)
     widen(2)
     widen(0)
     enter()
-    w_start(0, 8, 0, 1, 9, 10)
+    w_start(0, 0, 1)
     tiles(0, first_tile)
     widen_halo(1)
     widen_halo(2)
@@ -443,6 +445,7 @@
     tiles(1, mend_tile)
     tiles(1, combine_tile(1))
     states_out(1, 0)
+    w_start(0, 8, 4)
     widen_halo(0)
     states_in(0, 0)
     tiles(0, row_tile(0))
@@ -450,8 +453,8 @@
     states_in(1, 0)
     tiles(1, row_tile(1))
     states_out(1, 1)
-    w_start(0, 4)
-    w_start(1, 8, 4)
+    w_start(0, 9, 10)
+    w_own(1)
     states_in(0, 1)
     tiles(0, seed_tile(0))
     outputs(0)
@@ -459,11 +462,8 @@
     when(0, a_start, 0, 0, 1, 4)
     outputs(1)
     when(1, p_begin, 1)
-    when(0, a_start, 1, 0, 1, 4)
+    when(0, a_start, 1, 4)
     states_in(1, 1)
-    w_first(0)
-    w_start(1, 0, 1, 9, 10)
-    w_own(2)
     tiles(1, seed_tile(1))
     outputs(2)
     when(1, p_begin, 2)
@@ -473,54 +473,60 @@
     when(1, p_begin, 3)
     when(0, a_start, 3, 4)
     when(1, a_cross, 1)
-    acc[...] = jnp.zeros_like(acc)
+    w_first(0)
     when(1, a_middle, 0)
-    w_second(0)
     when(1, a_cross, 2)
     when(1, a_middle, 1)
     when(1, a_cross, 3)
     when(1, a_end, 0)
     when(1, a_middle, 2)
+    w_second(0)
     when(1, a_end, 1)
     when(1, a_middle, 3)
+    when(0, a_sibling, 3, 4)
     when(0, a_middle, 0)
-    when(0, a_middle, 1)
+    when(0, a_start, 1, 0, 1)
+    when(0, a_sibling, 0, 4, 5, 6, 7)
+    when(0, a_sibling, 1, 4, 5, 6)
     when(0, a_start, 2, 0, 1)
-    when(0, a_start, 3, 0, 1)
     w_first(1)
+    w_own(2)
     when(1, a_end, 2)
     when(1, a_end, 3)
+    when(0, a_sibling, 1, 7)
+    when(0, a_start, 3, 0, 1)
     w_third(0)
-    when(0, a_pair, 0)
-    when(0, a_pair, 1)
-    sweep(THEIRS, EVERY, (0, 1), (0, 1))
     when(0, a_pair, 2)
-    when(0, a_pair, 3)
-    sweep(THEIRS, EVERY, (1, 1), (0, 1))
+    when(0, a_sibling, 3, 5, 6, 7)
+    partial(0)
     c_begin(0)
+    partial(1)
+    c_begin(1)
+    when(0, a_middle, 1)
+    when(0, a_end, 0)
     w_second(1)
     when(0, a_middle, 2)
-    when(0, a_end, 0)
-    when(0, a_middle, 3)
     when(0, a_end, 1)
     w_first(2)
-    w_third(1)
-    sweep(THEIRS, EVERY, (0, 2), (1, 1))
-    c_begin(1)
-    sweep(THEIRS, EVERY, (0, 2), (2, 1))
+    when(0, a_middle, 3)
+    w_wait(1, 4, 5, 6)
+    prepare(cy, 2)
+    w_wait(1, 7, 11, 12, 15, 16)
+    finish(cy, 2)
     c_begin(2)
     when(0, a_end, 2)
     when(0, a_end, 3)
     w_second(2)
+    w_wait(2, 4, 5, 6)
+    prepare(cy, 3)
+    w_wait(2, 7, 11, 12, 15, 16)
+    finish(cy, 3)
+    c_begin(3)
     when(1, a_pair, 0)
     when(1, a_pair, 1)
     when(1, a_pair, 2)
     when(1, a_pair, 3)
-    sweep(OWN, EVERY, (0, 2), (0, 3))
-    w_third(2)
-    sweep(THEIRS, EVERY, (0, 2), (3, 1))
-    c_begin(3)
-    sweep(OWN, EVERY, (0, 2), (3, 1))
+    own(0, 4)
     for n in range(CHUNKS):
         c_end(n)
 
@@ -558,7 +564,8 @@
         scratch_shapes=[
             pltpu.VMEM((2 * SIDE, CHUNKS, ROWS, CHUNK), BF16),
             pltpu.VMEM((2 * SIDE + 1, PIECES, ROWS, PIECE), BF16),
-            pltpu.VMEM((2, CHUNKS, ROWS, CHUNK), F32),
+            pltpu.VMEM((CHUNKS, ROWS, CHUNK), F32),
+            pltpu.VMEM((CHUNKS, ROWS, CHUNK), F32),
             pltpu.VMEM((CHUNKS, ROWS, CHUNK), BF16),
             pltpu.VMEM((CHUNKS, ROWS, CHUNK), BF16),
             pltpu.VMEM((3, ROWS, WIDTH), BF16),

time: 95.5 us -> 86.9 us (0.910); the launches traced: 93.9 us -> 86.7 us
  Pallas kernels: 91.6 us -> 84.4 us
    pallas_call x1, Pallas kernels: 91.6 us -> 84.4 us  [per_device(): pl.pallas_call(kernel, out_shape=jax.ShapeDtypeStruct((ROWS, WIDTH), BF16...]
where the time goes in v4:
time: 86.9 us; the launch traced here: 86.7 us
  Pallas kernels  84.4 us (97%)
  local copies, waits for them, and re-layouts  2.26 us (3%)
    pallas_call x1, Pallas kernels, per_device(): pl.pallas_call(kernel, out_shape=jax.ShapeDtypeStruct((ROWS, WIDTH), BF16...  84.4 us
    unnamed x1, local copies, waits for them, and re-layouts  2.26 us

profile of v4, /device:TPU:1, one launch (start us, length us, event | category | flops | bytes accessed | tf_op | source)
XLA Modules:
  0.0 86.7 jit_solution(13060453140410615022)
XLA Ops:
  0.0 84.4 %shard_map.73 = bf16[512,1024]{1,0:T(8,128)(2,1)} custom-call(bf16[512,1024]{1,0:T(8,128)(2,1)} %q_hbm.1, bf16[512,1024]{1,0:T(8,128)(2,1)} %k_hbm.1, bf16[512,1024]{1,0:T(8,128)(2,1)} %v_hbm.1, f32[3,3,1024]{2,1,0:T(4,128)} %taps_ref.1, f32[16,1024]{1,0:T(8,128)} %rates_ref.1, f32[16,1024]{1,0:T(8,128)} %res_ref.1, bf16[512,1024]{1,0:T(8,128)(2,1)} %w_ref.1), custom_call_target="tpu_custom_call" | custom-call | flops 8589934592 | bytes 6291456 | tf_op jit(solution)/shard_map/pallas_call | solution.py:559
  84.4 2.3 %copy.9 = bf16[512,1024]{1,0:T(8,128)(2,1)} copy(bf16[512,1024]{1,0:T(8,128)(2,1)} %shard_map.73) | data formatting | bytes 2097152

commit v5 on v4

--- a/solution.py
+++ b/solution.py
@@ -432,7 +432,6 @@
 
     widen(1)
     widen(2)
-    widen(0)
     enter()
     w_start(0, 0, 1)
     tiles(0, first_tile)
@@ -446,6 +445,7 @@
     tiles(1, combine_tile(1))
     states_out(1, 0)
     w_start(0, 8, 4)
+    widen(0)
     widen_halo(0)
     states_in(0, 0)
     tiles(0, row_tile(0))
@@ -462,7 +462,7 @@
     when(0, a_start, 0, 0, 1, 4)
     outputs(1)
     when(1, p_begin, 1)
-    when(0, a_start, 1, 4)
+    when(0, a_start, 1, 0, 1, 4)
     states_in(1, 1)
     tiles(1, seed_tile(1))
     outputs(2)
@@ -483,9 +483,8 @@
     w_second(0)
     when(1, a_end, 1)
     when(1, a_middle, 3)
+    when(0, a_middle, 0)
     when(0, a_sibling, 3, 4)
-    when(0, a_middle, 0)
-    when(0, a_start, 1, 0, 1)
     when(0, a_sibling, 0, 4, 5, 6, 7)
     when(0, a_sibling, 1, 4, 5, 6)
     when(0, a_start, 2, 0, 1)

time: 86.9 us -> 86.6 us (level)
  no operation moved by 1% of the time
where the time goes in v5:
time: 86.6 us; the launch traced here: 86.4 us
  Pallas kernels  84.2 us (97%)
  local copies, waits for them, and re-layouts  2.26 us (3%)
    pallas_call x1, Pallas kernels, per_device(): pl.pallas_call(kernel, out_shape=jax.ShapeDtypeStruct((ROWS, WIDTH), BF16...  84.2 us
    unnamed x1, local copies, waits for them, and re-layouts  2.26 us

profile of v5, /device:TPU:1, one launch (start us, length us, event | category | flops | bytes accessed | tf_op | source)
XLA Modules:
  0.0 86.4 jit_solution(15841579468868037748)
XLA Ops:
  0.0 84.2 %shard_map.73 = bf16[512,1024]{1,0:T(8,128)(2,1)} custom-call(bf16[512,1024]{1,0:T(8,128)(2,1)} %q_hbm.1, bf16[512,1024]{1,0:T(8,128)(2,1)} %k_hbm.1, bf16[512,1024]{1,0:T(8,128)(2,1)} %v_hbm.1, f32[3,3,1024]{2,1,0:T(4,128)} %taps_ref.1, f32[16,1024]{1,0:T(8,128)} %rates_ref.1, f32[16,1024]{1,0:T(8,128)} %res_ref.1, bf16[512,1024]{1,0:T(8,128)(2,1)} %w_ref.1), custom_call_target="tpu_custom_call" | custom-call | flops 8589934592 | bytes 6291456 | tf_op jit(solution)/shard_map/pallas_call | solution.py:558
  84.2 2.3 %copy.9 = bf16[512,1024]{1,0:T(8,128)(2,1)} copy(bf16[512,1024]{1,0:T(8,128)(2,1)} %shard_map.73) | data formatting | bytes 2097152

commit v6 on v5

--- a/solution.py
+++ b/solution.py
@@ -342,7 +342,7 @@
         start = (strided(0, tile, PAD - 1), strided(0, tile, PAD - 2),
                  tuple(inits[tile, pl.ds(r, SEGS, stride=ORDER), :] for r in range(ORDER)))
         lax.fori_loop(0, STEPS, step, start, unroll=4)
-        abuf[target_block, tile // 2, :, lanes_of(tile % 2)] = ybuf[...].astype(BF16)
+        abuf[target_block, tile // 2, :, lanes_of(tile % 2)] = ybuf[pl.ds(0, ROWS), :].astype(BF16)
         return carry
 
     def tiles(part, body):
@@ -353,11 +353,11 @@
         lax.fori_loop(2 * q, 2 * q + 2, second_tile, 0)
 
     def states_out(part, stage):
-        for distance in (1, 3, 2):
+        for distance in (2, 1, 3):
             state_copy(part, stage, distance, False).start()
 
     def states_in(part, stage):
-        for distance in (1, 3, 2):
+        for distance in (2, 1, 3):
             state_copy(part, stage, distance, True).wait_recv()
 
     def when(wanted, call, *args):
@@ -568,13 +568,13 @@
             pltpu.VMEM((CHUNKS, ROWS, CHUNK), BF16),
             pltpu.VMEM((CHUNKS, ROWS, CHUNK), BF16),
             pltpu.VMEM((3, ROWS, WIDTH), BF16),
-            pltpu.VMEM((3, TILES, PAD + ROWS, LANES), F32),
+            pltpu.VMEM((3, TILES, PAD + ROWS + STEPS, LANES), F32),
             pltpu.VMEM((TILES, STEPS, SEGS, LANES), F32),
-            pltpu.VMEM((ROWS, LANES), F32),
+            pltpu.VMEM((ROWS + STEPS, LANES), F32),
             pltpu.VMEM((3, HALO, WIDTH), BF16),
             pltpu.VMEM((ORDER, WIDTH), F32),
-            pltpu.VMEM((TILES, SEGS * ORDER, LANES), F32),
-            pltpu.VMEM((TILES, SEGS * ORDER, LANES), F32),
+            pltpu.VMEM((TILES, (SEGS + 1) * ORDER, LANES), F32),
+            pltpu.VMEM((TILES, (SEGS + 1) * ORDER, LANES), F32),
             pltpu.VMEM((PARTS, SIDE, ORDER, PART), F32),
             pltpu.VMEM((PARTS, SIDE, ORDER, PART), F32),
             dma((len(GROUPS) * PER_GROUP,)), dma((len(GROUPS) * PER_GROUP,)),

time: 86.6 us -> 86.5 us (level)
  no operation moved by 1% of the time
where the time goes in v6:
time: 86.5 us; the launch traced here: 86.3 us
  Pallas kernels  84 us (97%)
  local copies, waits for them, and re-layouts  2.26 us (3%)
    pallas_call x1, Pallas kernels, per_device(): pl.pallas_call(kernel, out_shape=jax.ShapeDtypeStruct((ROWS, WIDTH), BF16...  84 us
    unnamed x1, local copies, waits for them, and re-layouts  2.26 us

profile of v6, /device:TPU:1, one launch (start us, length us, event | category | flops | bytes accessed | tf_op | source)
XLA Modules:
  0.0 86.3 jit_solution(9369407944140330563)
XLA Ops:
  0.0 84.0 %shard_map.73 = bf16[512,1024]{1,0:T(8,128)(2,1)} custom-call(bf16[512,1024]{1,0:T(8,128)(2,1)} %q_hbm.1, bf16[512,1024]{1,0:T(8,128)(2,1)} %k_hbm.1, bf16[512,1024]{1,0:T(8,128)(2,1)} %v_hbm.1, f32[3,3,1024]{2,1,0:T(4,128)} %taps_ref.1, f32[16,1024]{1,0:T(8,128)} %rates_ref.1, f32[16,1024]{1,0:T(8,128)} %res_ref.1, bf16[512,1024]{1,0:T(8,128)(2,1)} %w_ref.1), custom_call_target="tpu_custom_call" | custom-call | flops 8589934592 | bytes 6291456 | tf_op jit(solution)/shard_map/pallas_call | solution.py:558
  84.0 2.3 %copy.9 = bf16[512,1024]{1,0:T(8,128)(2,1)} copy(bf16[512,1024]{1,0:T(8,128)(2,1)} %shard_map.73) | data formatting | bytes 2097152

commit v7 on v6

--- a/solution.py
+++ b/solution.py
@@ -251,7 +251,7 @@
         zero = jnp.zeros((SEGS, LANES), F32)
         start = (strided(1, tile, PAD - 1), strided(1, tile, PAD - 2),
                  strided(2, tile, PAD - 1), strided(2, tile, PAD - 2), (zero,) * ORDER)
-        states = lax.fori_loop(0, STEPS, step, start, unroll=4)[4]
+        states = lax.fori_loop(0, STEPS, step, start, unroll=8)[4]
         for r in range(ORDER):
             ends[tile, pl.ds(r, SEGS, stride=ORDER), :] = states[r]
         return carry
@@ -341,7 +341,7 @@
 
         start = (strided(0, tile, PAD - 1), strided(0, tile, PAD - 2),
                  tuple(inits[tile, pl.ds(r, SEGS, stride=ORDER), :] for r in range(ORDER)))
-        lax.fori_loop(0, STEPS, step, start, unroll=4)
+        lax.fori_loop(0, STEPS, step, start, unroll=8)
         abuf[target_block, tile // 2, :, lanes_of(tile % 2)] = ybuf[pl.ds(0, ROWS), :].astype(BF16)
         return carry
 

time: 86.5 us -> 86.3 us (level)
  no operation moved by 1% of the time
where the time goes in v7:
time: 86.3 us; the launch traced here: 85.9 us
  Pallas kernels  83.6 us (97%)
  local copies, waits for them, and re-layouts  2.26 us (3%)
    pallas_call x1, Pallas kernels, per_device(): pl.pallas_call(kernel, out_shape=jax.ShapeDtypeStruct((ROWS, WIDTH), BF16...  83.6 us
    unnamed x1, local copies, waits for them, and re-layouts  2.26 us

profile of v7, /device:TPU:1, one launch (start us, length us, event | category | flops | bytes accessed | tf_op | source)
XLA Modules:
  0.0 85.9 jit_solution(16414739249142813135)
XLA Ops:
  0.0 83.6 %shard_map.73 = bf16[512,1024]{1,0:T(8,128)(2,1)} custom-call(bf16[512,1024]{1,0:T(8,128)(2,1)} %q_hbm.1, bf16[512,1024]{1,0:T(8,128)(2,1)} %k_hbm.1, bf16[512,1024]{1,0:T(8,128)(2,1)} %v_hbm.1, f32[3,3,1024]{2,1,0:T(4,128)} %taps_ref.1, f32[16,1024]{1,0:T(8,128)} %rates_ref.1, f32[16,1024]{1,0:T(8,128)} %res_ref.1, bf16[512,1024]{1,0:T(8,128)(2,1)} %w_ref.1), custom_call_target="tpu_custom_call" | custom-call | flops 8589934592 | bytes 6291456 | tf_op jit(solution)/shard_map/pallas_call | solution.py:558
  83.6 2.3 %copy.9 = bf16[512,1024]{1,0:T(8,128)(2,1)} copy(bf16[512,1024]{1,0:T(8,128)(2,1)} %shard_map.73) | data formatting | bytes 2097152
